TPU v7x, 32 devices: a whole 2x2x4 slice. The times are simulated.
32 devices in a mesh: groups: 2 (over y), dp: 4 (over z), feat: 2 (over core), ens: 2 (over x).
Axes of the slice: x: 2, y: 2, z: 4, core: 2. Of those that a mesh axis runs over, the one named last changes fastest.
Arguments:
- test_feat: bfloat16 [2, 64, 8192], P('ens', 'groups', 'dp'), parts along dimension 1, may hold values from -6 to 6
- kernel_inverse: bfloat16 [2, 8192, 8192], P('ens', 'dp', 'feat'), may hold values from -0.0625 to 0.0625
- train_feat: bfloat16 [2, 1024, 8192], P('ens', 'dp', 'feat'), may hold values from -0.0625 to 0.0625
- residual_weight: float32 [2, 1024], P('ens', 'dp'), may hold values from 0.05 to 1
Outputs:
- scores: float32 [64, 1024], P(('groups', 'feat', 'ens'), 'dp'), parts along dimension 0
There are 2 independent parts, one for each index of `groups`. A program takes and returns all parts, laid end to end along the dimension named above; an argument that names none is the same for every part. Nothing has to cross between parts.
All inputs are finite; a program needn't handle non-finite values.
Results may differ from a plain program's by a relative error of at most 0.0029.
Values may be sent and summed in bfloat16 or wider, within the bound.
No kernel may reach another device: no remote copies, remote signals or barrier semaphores. Data moves between devices by JAX's collectives and lax.ppermute only.
A program may use at most 64 MiB of HBM per device.

v0:
```python
import jax
import jax.numpy as jnp
from jax import lax
from jax.sharding import PartitionSpec as P


def shards(test_feat, kernel_inverse, train_feat, residual_weight):
    test_local = test_feat[0]
    inverse_local = kernel_inverse[0]
    train_local = train_feat[0]
    weight_row = residual_weight[0][None, :]
    partial_sum = jnp.dot(test_local, inverse_local, preferred_element_type=jnp.float32)
    projected = lax.psum(partial_sum, "dp").astype(jnp.bfloat16)
    raw = jnp.einsum("tf,nf->tn", projected, train_local, preferred_element_type=jnp.float32)
    totals = raw * weight_row
    return lax.psum_scatter(totals, ("feat", "ens"), scatter_dimension=0, tiled=True)


def solution(mesh):
    in_specs = (
        P("ens", "groups", "dp"),
        P("ens", "dp", "feat"),
        P("ens", "dp", "feat"),
        P("ens", "dp"),
    )
    out_specs = P(("groups", "feat", "ens"), "dp")
    return jax.shard_map(shards, mesh=mesh, in_specs=in_specs, out_specs=out_specs, check_vma=False)
```

profile of v0, /device:TPU:0, one launch (start us, length us, event | category | flops | bytes accessed | tf_op | source)
XLA Modules:
  0.0 73.9 jit_solution(5447746823196072305)
XLA Ops:
  6.5 0.0 copy-start
  6.5 0.0 copy-start.1
  6.5 0.0 reduce-scatter.2.cloned.1.call-start
  6.5 9.0 %fusion = f32[32,4096]{1,0:T(8,128)S(1)} fusion(bf16[1,2048,4096]{2,1,0:T(8,128)(2,1)} %param.5, bf16[1,32,2048]{2,1,0:T(8,128)(2,1)} %param.4), kind=kOutput, calls=%fused_computation | convolution fusion | flops 536870912 | bytes 17432576 | tf_op jit(solution)/shard_map/dot_general | solution.py:12
  15.5 32.1 %all-reduce.1 = bf16[32,4096]{1,0:T(8,128)(2,1)S(1)} all-reduce(f32[32,4096]{1,0:T(8,128)S(1)} %fusion), channel_id=1, replica_groups=mesh['groups'=2,'dp'=4,'feat'=2,'ens'=2] {'dp'}, use_global_device_ids=true, to_apply=%region_0.0 | all-reduce | flops 131072 | bytes 786432 | tf_op jit(solution)/shard_map/psum | solution.py:13
  47.6 0.0 copy-done
  47.6 0.0 copy-done.1
  47.6 1.3 %fusion.4 = f32[32,256]{1,0:T(8,128)} fusion(bf16[1,256,4096]{2,1,0:T(8,128)(2,1)S(1)} %copy-done, bf16[32,4096]{1,0:T(8,128)(2,1)S(1)} %all-reduce.1, f32[256]{0:T(256)S(1)} %bitcast.13), kind=kOutput, calls=%fused_computation.4 | convolution fusion | flops 67117056 | bytes 2393088 | tf_op jit(solution)/shard_map/tf,nf->tn/dot_general | solution.py:14
  49.0 0.0 reduce-scatter.2.cloned.1.call-update
  49.0 18.0 %reduce-scatter.2.cloned.1.call-done = f32[8,256]{1,0:T(8,128)} async-done(((f32[32,256]{1,0:T(8,128)}), f32[8,256]{1,0:T(8,128)}) %reduce-scatter.2.cloned.1.call-update) | async-done | bytes 8208 | tf_op jit(solution)/shard_map/reduce_scatter | solution.py:16
Async XLA Ops:
  6.5 41.1 %copy-start = (bf16[1,256,4096]{2,1,0:T(8,128)(2,1)S(1)}, bf16[1,256,4096]{2,1,0:T(8,128)(2,1)}, u32[]{:S(2)}) copy-start(bf16[1,256,4096]{2,1,0:T(8,128)(2,1)} %param.6) | copy-start | bytes 6291460
  6.5 41.1 %copy-start.1 = (f32[1,256]{1,0:T(1,128)S(1)}, f32[1,256]{1,0:T(1,128)}, u32[]{:S(2)}) copy-start(f32[1,256]{1,0:T(1,128)} %param.7) | copy-start | bytes 3076
  6.5 60.5 %reduce-scatter.2.cloned.1.call-start = ((), (), s32[]{:S(2)}) async-start(), calls=%async_computation.1 | async-start | bytes 40960 | tf_op jit(solution)/shard_map/reduce_scatter | solution.py:16
Sparse Core Ops, SparseCore 0:
  49.1 17.8 reduce-scatter.1
where the time goes:
time: 74 us; the launch traced here: 73.9 us
  blocking collectives  32.1 us (43%)
  waiting for transfers between devices  18 us (24%)
  between operations  13.4 us (18%)
  matrix products  10.3 us (14%)
    psum x1, blocking collectives, shards(): projected = lax.psum(partial_sum, 'dp').astype(jnp.bfloat16)  32.1 us
    reduce_scatter x1, waiting for transfers between devices, shards(): lax.psum_scatter(totals, ('feat', 'ens'), scatter_dimension=0, tiled=True)  18 us
    dot_general x1, matrix products, shards(): jnp.dot(test_local, inverse_local, preferred_element_type=jnp.float32)  8.96 us
  transfers between devices with their start and end apart: 1, of which 1 were waited for; matrix products, arithmetic and copies ran while one was open for 0% of the time, Pallas kernels for 0%

commit v1 on v0

v1 whole, which is shorter than its diff:
```python
import functools

import jax
import jax.numpy as jnp
from jax import lax
from jax.experimental import pallas as pl
from jax.experimental.pallas import tpu as pltpu
from jax.sharding import PartitionSpec as P

VMEM = pl.BlockSpec(memory_space=pltpu.VMEM)
HBM = pl.BlockSpec(memory_space=pltpu.HBM)


def place(n):
    z = lax.axis_index("dp")
    near = (z >= n // 2).astype(jnp.int32)
    hub = (z == n // 2 - 1) | (z == n // 2)
    return hub, near


def half_kernel(n, who, chunks, test_ref, inverse_ref, out_ref, test_buf, buf, total, test_sem, sems):
    hub, near = place(n)
    if who == "ends":
        active, half = jnp.logical_not(hub), 1 - near
    elif who == "hubs":
        active, half = hub, near
    else:
        active, half = None, jnp.where(hub, 1 - near, near)
    rows, width = buf.shape[1:]

    def run():
        columns = pl.ds(pl.multiple_of(half * width, width), width)
        test_copy = pltpu.make_async_copy(test_ref.at[0], test_buf, test_sem)
        test_copy.start()
        copies = [
            pltpu.make_async_copy(inverse_ref.at[0, pl.ds(c * rows, rows), columns], buf.at[c], sems.at[c])
            for c in range(chunks)
        ]
        for copy in copies:
            copy.start()
        test_copy.wait()
        for c in range(chunks):
            copies[c].wait()
            term = jnp.dot(test_buf[:, c * rows : (c + 1) * rows], buf[c], preferred_element_type=jnp.float32)
            if c:
                term = total[...] + term
            if c < chunks - 1:
                total[...] = term
            else:
                out_ref[...] = term.astype(out_ref.dtype)

    if active is None:
        run()
    else:
        pl.when(active)(run)


def half_dot(n, who, out_dtype, test, inverse):
    tests, depth = test.shape[1:]
    width = inverse.shape[2] // 2
    rows = min(depth, 256)
    chunks = depth // rows
    return pl.pallas_call(
        functools.partial(half_kernel, n, who, chunks),
        in_specs=[HBM, HBM],
        out_specs=VMEM,
        out_shape=jax.ShapeDtypeStruct((tests, width), out_dtype),
        scratch_shapes=[
            pltpu.VMEM((tests, depth), test.dtype),
            pltpu.VMEM((chunks, rows, width), inverse.dtype),
            pltpu.VMEM((tests, width), jnp.float32),
            pltpu.SemaphoreType.DMA,
            pltpu.SemaphoreType.DMA((chunks,)),
        ],
        compiler_params=pltpu.CompilerParams(vmem_limit_bytes=52 * 2**20),
        cost_estimate=pl.CostEstimate(
            flops=2 * tests * depth * width, bytes_accessed=2 * depth * width, transcendentals=0
        ),
        name="half_" + who,
    )(test, inverse)


def score_kernel(n, parts, sum_ref, across_ref, back_ref, far_ref, train_ref, weight_ref, *rest):
    outs, raw, near_buf, far_buf = rest[:parts], rest[parts], rest[parts + 1], rest[parts + 2]
    hub, near = place(n)
    width = sum_ref.shape[1]

    def halves(near_half, far_half):
        def run():
            near_buf[...] = near_half[...]
            far_buf[...] = far_half[...]

        return run

    pl.when(hub)(halves(sum_ref, across_ref))
    pl.when(jnp.logical_not(hub))(halves(back_ref, far_ref))
    contract = (((1,), (1,)), ((), ()))

    def half_score(values, half):
        columns = pl.ds(pl.multiple_of(half * width, width), width)
        return lax.dot_general(values[...], train_ref[0, :, columns], contract, preferred_element_type=jnp.float32)

    raw[...] = (half_score(near_buf, near) + half_score(far_buf, 1 - near)) * weight_ref[...]
    me = lax.axis_index("feat")
    rows = outs[0].shape[0]
    for step, out in enumerate(outs):
        block = lax.rem(me + step, parts)
        out[...] = raw[pl.ds(pl.multiple_of(block * rows, rows), rows), :]


def score(n, parts, total, across, back, far, train, weight):
    tests, width = total.shape
    columns = train.shape[1]
    return pl.pallas_call(
        functools.partial(score_kernel, n, parts),
        in_specs=[VMEM] * 6,
        out_specs=[VMEM] * parts,
        out_shape=[jax.ShapeDtypeStruct((tests // parts, columns), jnp.float32)] * parts,
        scratch_shapes=[
            pltpu.VMEM((tests, columns), jnp.float32),
            pltpu.VMEM((tests, width), total.dtype),
            pltpu.VMEM((tests, width), total.dtype),
        ],
        compiler_params=pltpu.CompilerParams(vmem_limit_bytes=16 * 2**20),
        cost_estimate=pl.CostEstimate(
            flops=4 * tests * columns * width, bytes_accessed=4 * columns * width, transcendentals=0
        ),
        name="score",
    )(total, across, back, far, train, weight)


def split_kernel(axis, parts, *refs):
    terms, outs, total = refs[: -parts - 1], refs[-parts - 1 : -1], refs[-1]
    value = terms[0][...]
    for term in terms[1:]:
        value = value + term[...]
    total[...] = value
    me = lax.axis_index(axis)
    rows = outs[0].shape[0]
    for step, out in enumerate(outs):
        block = lax.rem(me + step, parts)
        out[...] = total[pl.ds(pl.multiple_of(block * rows, rows), rows), :]


def add_and_split(axis, parts, terms):
    rows, columns = terms[0].shape
    return pl.pallas_call(
        functools.partial(split_kernel, axis, parts),
        in_specs=[VMEM] * len(terms),
        out_specs=[VMEM] * parts,
        out_shape=[jax.ShapeDtypeStruct((rows // parts, columns), jnp.float32)] * parts,
        scratch_shapes=[pltpu.VMEM((rows, columns), jnp.float32)],
        compiler_params=pltpu.CompilerParams(vmem_limit_bytes=4 * 2**20),
        name="add_and_split",
    )(*terms)


def exchange(axis, parts, blocks):
    received = [
        lax.ppermute(block, axis, [(i, (i + step) % parts) for i in range(parts)])
        for step, block in list(enumerate(blocks))[1:]
    ]
    return [blocks[0], *received]


def line_shards(n, feats, models, test_feat, kernel_inverse, train_feat, residual_weight):
    left, right = n // 2 - 1, n // 2
    ends_far = half_dot(n, "ends", jnp.bfloat16, test_feat, kernel_inverse)
    far_in = [lax.ppermute(ends_far, "dp", [(left - m, right), (right + m, left)]) for m in range(1, left + 1)]
    second = half_dot(n, "both", jnp.bfloat16, test_feat, kernel_inverse)
    across_in = lax.ppermute(second, "dp", [(left, right), (right, left)])
    near_in = [lax.ppermute(second, "dp", [(left - m, left), (right + m, right)]) for m in range(1, left + 1)]
    own = half_dot(n, "hubs", jnp.float32, test_feat, kernel_inverse)
    total = own
    for term in [*far_in, across_in, *near_in]:
        total = total + term
    total = total.astype(jnp.bfloat16)
    far_out = [lax.ppermute(total, "dp", [(left, right + m), (right, left - m)]) for m in range(1, left + 1)]
    near_out = [lax.ppermute(total, "dp", [(left, left - m), (right, right + m)]) for m in range(1, left + 1)]
    across_out = lax.ppermute(total, "dp", [(left, right), (right, left)])
    blocks = score(n, feats, total, across_out, sum(near_out), sum(far_out), train_feat, residual_weight)
    terms = exchange("feat", feats, blocks)
    blocks = add_and_split("ens", models, terms)
    terms = exchange("ens", models, blocks)
    result = terms[0]
    for term in terms[1:]:
        result = result + term
    return result


def general_shards(test_feat, kernel_inverse, train_feat, residual_weight):
    partial_sum = jnp.dot(test_feat[0], kernel_inverse[0], preferred_element_type=jnp.float32)
    projected = lax.psum(partial_sum, "dp").astype(jnp.bfloat16)
    raw = jnp.einsum("tf,nf->tn", projected, train_feat[0], preferred_element_type=jnp.float32)
    totals = raw * residual_weight[0][None, :]
    return lax.psum_scatter(totals, ("feat", "ens"), scatter_dimension=0, tiled=True)


def solution(mesh):
    in_specs = (
        P("ens", "groups", "dp"),
        P("ens", "dp", "feat"),
        P("ens", "dp", "feat"),
        P("ens", "dp"),
    )
    out_specs = P(("groups", "feat", "ens"), "dp")
    line = mesh.shape["dp"]
    if line % 2 == 0 and line // 2 - 1 == 1:
        body = functools.partial(line_shards, line, mesh.shape["feat"], mesh.shape["ens"])
    else:
        body = general_shards
    return jax.shard_map(body, mesh=mesh, in_specs=in_specs, out_specs=out_specs, check_vma=False)
```

time: 74 us -> 34.3 us (0.46)
  blocking collectives: 32.1 us -> 0 us
  between operations: 13.4 us -> 0.12 us
  matrix products: 10.3 us -> 0 us
  starting transfers between devices: 0.01 us -> 9.04 us
  Pallas kernels: 0 us -> 8.74 us
  waiting for transfers between devices: 18 us -> 14.5 us
  local copies, waits for them, and re-layouts: 0.01 us -> 0.92 us
    psum x1 -> x0, blocking collectives: 32.1 us -> none  [shards(): projected = lax.psum(partial_sum, 'dp').astype(jnp.bfloat16)]
    reduce_scatter x1 -> x0, waiting for transfers between devices: 18 us -> none  [shards(): lax.psum_scatter(totals, ('feat', 'ens'), scatter_dimension=0, tiled=True)]
    ppermute x0 -> x8, waiting for transfers between devices: none -> 14.5 us  [the longest x1 6.5 us: line_shards(): lax.ppermute(total, 'dp', [(left, right + m), (right, left - m)])]
    dot_general x2 -> x0, matrix products: 10.3 us -> none  [the longest x1 8.96 us: shards(): jnp.dot(test_local, inverse_local, preferred_element_type=jnp.float32)]
    ppermute x0 -> x8, starting transfers between devices: none -> 9.04 us  [the longest x1 2.25 us: line_shards(): lax.ppermute(ends_far, 'dp', [(left - m, right), (right + m, left)])]
    pallas_call x0 -> x5, Pallas kernels: none -> 8.74 us  [the longest x3 7.96 us: half_dot(): pl.pallas_call(functools.partial(half_kernel, n, who, chunks), in_specs=[...]
    unnamed x4 -> x6, local copies, waits for them, and re-layouts: 0.01 us -> 0.92 us
  transfers between devices with their start and end apart: 1 -> 8, of which waited for: 1 -> 5; matrix products, arithmetic and copies ran while one was open for 0% -> 0% of each run, Pallas kernels for 0% -> 12%
where the time goes in v1:
time: 34.3 us; the launch traced here: 34 us
  waiting for transfers between devices  14.5 us (42%)
  starting transfers between devices  9.04 us (26%)
  Pallas kernels  8.74 us (25%)
  local copies, waits for them, and re-layouts  0.92 us (3%)
  other arithmetic  0.67 us (2%)
    pallas_call x3, Pallas kernels, half_dot(): pl.pallas_call(functools.partial(half_kernel, n, who, chunks), in_specs=[...  7.96 us
    ppermute x1, waiting for transfers between devices, line_shards(): lax.ppermute(total, 'dp', [(left, right + m), (right, left - m)])  6.5 us
    ppermute x2, waiting for transfers between devices, exchange(): lax.ppermute(block, axis, [(i, (i + step) % parts) for i in range(parts)])  3.33 us
    ppermute x1, waiting for transfers between devices, line_shards(): lax.ppermute(total, 'dp', [(left, left - m), (right, right + m)])  2.7 us
    ppermute x1, starting transfers between devices, line_shards(): lax.ppermute(ends_far, 'dp', [(left - m, right), (right + m, left)])  2.25 us
    ppermute x1, waiting for transfers between devices, line_shards(): lax.ppermute(second, 'dp', [(left - m, left), (right + m, right)])  2.01 us
    ppermute x2, starting transfers between devices, exchange(): lax.ppermute(block, axis, [(i, (i + step) % parts) for i in range(parts)])  1.57 us
    ppermute x1, starting transfers between devices, line_shards(): lax.ppermute(second, 'dp', [(left - m, left), (right + m, right)])  1.3 us
  transfers between devices with their start and end apart: 8, of which 5 were waited for; matrix products, arithmetic and copies ran while one was open for 0% of the time, Pallas kernels for 12%

profile of v1, /device:TPU:0, one launch (start us, length us, event | category | flops | bytes accessed | tf_op | source)
XLA Modules:
  0.0 34.0 jit_solution(590323163302045974)
XLA Ops:
  0.0 0.9 %copy-done.1 = bf16[1,32,2048]{2,1,0:T(8,128)(2,1)S(1)} copy-done((bf16[1,32,2048]{2,1,0:T(8,128)(2,1)S(1)}, bf16[1,32,2048]{2,1,0:T(8,128)(2,1)}, u32[]{:S(2)}) %copy-start.1) | copy-done | bytes 131096
  0.9 3.9 %half_ends.1 = bf16[32,2048]{1,0:T(8,128)(2,1)S(1)} custom-call(bf16[1,32,2048]{2,1,0:T(8,128)(2,1)S(1)} %copy-done.1, bf16[1,2048,4096]{2,1,0:T(8,128)(2,1)} %inverse_ref.5), custom_call_target="tpu_custom_call" | custom-call | flops 268435456 | bytes 8388608 | tf_op jit(solution)/shard_map/half_ends/pallas_call | solution.py:63
  4.8 0.0 copy-start
  4.8 0.0 copy-start.2
  4.8 2.3 %collective-permute-start = (bf16[32,2048]{1,0:T(8,128)(2,1)S(1)}, bf16[32,2048]{1,0:T(8,128)(2,1)S(1)}, u32[]{:S(2)}, u32[]{:S(2)}) collective-permute-start(bf16[32,2048]{1,0:T(8,128)(2,1)S(1)} %half_ends.1), channel_id=1, source_target_pairs={{0,8},{12,4},{1,9},{13,5},{2,10},{14,6},{3,11},{15,7},{16,24},{28,... | collective-permute-start | bytes 393224 | tf_op jit(solution)/shard_map/ppermute | solution.py:169
  7.1 4.0 %half_both.1 = bf16[32,2048]{1,0:T(8,128)(2,1)S(1)} custom-call(bf16[1,32,2048]{2,1,0:T(8,128)(2,1)S(1)} %copy-done.1, bf16[1,2048,4096]{2,1,0:T(8,128)(2,1)} %inverse_ref.5), custom_call_target="tpu_custom_call" | custom-call | flops 268435456 | bytes 8388608 | tf_op jit(solution)/shard_map/half_both/pallas_call | solution.py:63
  11.1 1.3 %collective-permute-start.2 = (bf16[32,2048]{1,0:T(8,128)(2,1)S(1)}, bf16[32,2048]{1,0:T(8,128)(2,1)S(1)}, u32[]{:S(2)}, u32[]{:S(2)}) collective-permute-start(bf16[32,2048]{1,0:T(8,128)(2,1)S(1)} %half_both.1), channel_id=1, source_target_pairs={{0,4},{12,8},{1,5},{13,9},{2,6},{14,10},{3,7},{15,11},{16,20},{28,... | collective-permute-start | bytes 393224 | tf_op jit(solution)/shard_map/ppermute | solution.py:172
  12.4 0.7 %collective-permute-start.1 = (bf16[32,2048]{1,0:T(8,128)(2,1)S(1)}, bf16[32,2048]{1,0:T(8,128)(2,1)S(1)}, u32[]{:S(2)}, u32[]{:S(2)}) collective-permute-start(bf16[32,2048]{1,0:T(8,128)(2,1)S(1)} %half_both.1), channel_id=1, source_target_pairs={{4,8},{8,4},{5,9},{9,5},{6,10},{10,6},{7,11},{11,7},{20,24},{24,20... | collective-permute-start | bytes 393224 | tf_op jit(solution)/shard_map/ppermute | solution.py:171
  13.1 0.1 half_hubs.1
  13.2 0.0 collective-permute-done
  13.2 2.0 %collective-permute-done.2 = bf16[32,2048]{1,0:T(8,128)(2,1)S(1)} collective-permute-done((bf16[32,2048]{1,0:T(8,128)(2,1)S(1)}, bf16[32,2048]{1,0:T(8,128)(2,1)S(1)}, u32[]{:S(2)}, u32[]{:S(2)}) %collective-permute-start.2) | collective-permute-done | bytes 131104 | tf_op jit(solution)/shard_map/ppermute | solution.py:172
  15.2 0.0 collective-permute-done.1
  15.2 0.1 add_convert_fusion.sum_ref
  15.3 1.3 %collective-permute-start.5 = (bf16[32,2048]{1,0:T(8,128)(2,1)S(1)}, bf16[32,2048]{1,0:T(8,128)(2,1)S(1)}, u32[]{:S(2)}, u32[]{:S(2)}) collective-permute-start(bf16[32,2048]{1,0:T(8,128)(2,1)S(1)} %add_convert_fusion.sum_ref), channel_id=1, source_target_pairs={{4,12},{8,0},{5,13},{9,1},{6,14},{10,2},{7,15},{11,3},{20,28},{24,... | collective-permute-start | bytes 393224 | tf_op jit(solution)/shard_map/ppermute | solution.py:178
  16.6 1.3 %collective-permute-start.4 = (bf16[32,2048]{1,0:T(8,128)(2,1)S(1)}, bf16[32,2048]{1,0:T(8,128)(2,1)S(1)}, u32[]{:S(2)}, u32[]{:S(2)}) collective-permute-start(bf16[32,2048]{1,0:T(8,128)(2,1)S(1)} %add_convert_fusion.sum_ref), channel_id=1, source_target_pairs={{4,0},{8,12},{5,1},{9,13},{6,2},{10,14},{7,3},{11,15},{20,16},{24,... | collective-permute-start | bytes 393224 | tf_op jit(solution)/shard_map/ppermute | solution.py:179
  17.9 0.7 %collective-permute-start.3 = (bf16[32,2048]{1,0:T(8,128)(2,1)S(1)}, bf16[32,2048]{1,0:T(8,128)(2,1)S(1)}, u32[]{:S(2)}, u32[]{:S(2)}) collective-permute-start(bf16[32,2048]{1,0:T(8,128)(2,1)S(1)} %add_convert_fusion.sum_ref), channel_id=1, source_target_pairs={{4,8},{8,4},{5,9},{9,5},{6,10},{10,6},{7,11},{11,7},{20,24},{24,20... | collective-permute-start | bytes 393224 | tf_op jit(solution)/shard_map/ppermute | solution.py:180
  18.5 6.5 %collective-permute-done.5.far_ref = bf16[32,2048]{1,0:T(8,128)(2,1)S(1)} collective-permute-done((bf16[32,2048]{1,0:T(8,128)(2,1)S(1)}, bf16[32,2048]{1,0:T(8,128)(2,1)S(1)}, u32[]{:S(2)}, u32[]{:S(2)}) %collective-permute-start.5) | collective-permute-done | bytes 131104 | tf_op jit(solution)/shard_map/ppermute | solution.py:178
  25.0 2.7 %collective-permute-done.4.back_ref = bf16[32,2048]{1,0:T(8,128)(2,1)S(1)} collective-permute-done((bf16[32,2048]{1,0:T(8,128)(2,1)S(1)}, bf16[32,2048]{1,0:T(8,128)(2,1)S(1)}, u32[]{:S(2)}, u32[]{:S(2)}) %collective-permute-start.4) | collective-permute-done | bytes 131104 | tf_op jit(solution)/shard_map/ppermute | solution.py:179
  27.7 0.8 %score.1 = (f32[16,256]{1,0:T(8,128)S(1)}, f32[16,256]{1,0:T(8,128)S(1)}) custom-call(bf16[32,2048]{1,0:T(8,128)(2,1)S(1)} %add_convert_fusion.sum_ref, bf16[32,2048]{1,0:T(8,128)(2,1)S(1)} %collective-permute-done.3.across_ref, bf16[32,2048]{1,0:T(8,128)(2,1)S(1)} %collective-permute-done.4.back_ref, bf16[32,2048]{1,0:T(8,128)(2,1)S(1)} %collective-permute-done.5.far_ref, ...), custom_call_target="tpu_custom_call" | custom-call | flops 67108864 | bytes 2097152 | tf_op jit(solution)/shard_map/score/pallas_call | solution.py:114
  28.5 0.1 collective-permute-start.6
  28.6 1.2 %collective-permute-done.6.refs_1_ = f32[16,256]{1,0:T(8,128)S(1)} collective-permute-done((f32[16,256]{1,0:T(8,128)S(1)}, f32[16,256]{1,0:T(8,128)S(1)}, u32[]{:S(2)}, u32[]{:S(2)}) %collective-permute-start.6) | collective-permute-done | bytes 16416 | tf_op jit(solution)/shard_map/ppermute | solution.py:160
  29.8 1.5 %collective-permute-start.7 = (f32[8,256]{1,0:T(8,128)S(1)}, f32[8,256]{1,0:T(8,128)S(1)}, u32[]{:S(2)}, u32[]{:S(2)}) collective-permute-start(f32[8,256]{1,0:T(8,128)S(1)} %get-tuple-element.12), channel_id=1, source_target_pairs={{0,1},{1,0},{2,3},{3,2},{4,5},{5,4},{6,7},{7,6},{8,9},{9,8},{10,11... | collective-permute-start | bytes 24584 | tf_op jit(solution)/shard_map/ppermute | solution.py:160
  31.3 2.2 %collective-permute-done.7 = f32[8,256]{1,0:T(8,128)S(1)} collective-permute-done((f32[8,256]{1,0:T(8,128)S(1)}, f32[8,256]{1,0:T(8,128)S(1)}, u32[]{:S(2)}, u32[]{:S(2)}) %collective-permute-start.7) | collective-permute-done | bytes 8224 | tf_op jit(solution)/shard_map/ppermute | solution.py:160
  33.4 0.6 %add.15 = f32[8,256]{1,0:T(8,128)} add(f32[8,256]{1,0:T(8,128)S(1)} %get-tuple-element.11, f32[8,256]{1,0:T(8,128)S(1)} %collective-permute-done.7) | non-fusion elementwise | flops 2048 | bytes 24576 | tf_op jit(solution)/shard_map/add | solution.py:187
  (5 shorter events, 0.0 us)
Async XLA Ops:
  0.0 0.9 %copy-start.1 = (bf16[1,32,2048]{2,1,0:T(8,128)(2,1)S(1)}, bf16[1,32,2048]{2,1,0:T(8,128)(2,1)}, u32[]{:S(2)}) copy-start(bf16[1,32,2048]{2,1,0:T(8,128)(2,1)} %test_ref.5) | copy-start | bytes 393220
  4.8 22.9 %copy-start = (bf16[1,256,4096]{2,1,0:T(8,128)(2,1)S(1)}, bf16[1,256,4096]{2,1,0:T(8,128)(2,1)}, u32[]{:S(2)}) copy-start(bf16[1,256,4096]{2,1,0:T(8,128)(2,1)} %train_ref.1) | copy-start | bytes 6291460
  4.8 22.9 %copy-start.2 = (f32[1,256]{1,0:T(1,128)S(1)}, f32[1,256]{1,0:T(1,128)}, u32[]{:S(2)}) copy-start(f32[1,256]{1,0:T(1,128)} %weight_ref.1) | copy-start | bytes 3076
  4.8 8.3 %collective-permute-start = (bf16[32,2048]{1,0:T(8,128)(2,1)S(1)}, bf16[32,2048]{1,0:T(8,128)(2,1)S(1)}, u32[]{:S(2)}, u32[]{:S(2)}) collective-permute-start(bf16[32,2048]{1,0:T(8,128)(2,1)S(1)} %half_ends.1), channel_id=1, source_target_pairs={{0,8},{12,4},{1,9},{13,5},{2,10},{14,6},{3,11},{15,7},{16,24},{28,... | collective-permute-start | bytes 393224 | tf_op jit(solution)/shard_map/ppermute | solution.py:169
  11.1 4.1 %collective-permute-start.2 = (bf16[32,2048]{1,0:T(8,128)(2,1)S(1)}, bf16[32,2048]{1,0:T(8,128)(2,1)S(1)}, u32[]{:S(2)}, u32[]{:S(2)}) collective-permute-start(bf16[32,2048]{1,0:T(8,128)(2,1)S(1)} %half_both.1), channel_id=1, source_target_pairs={{0,4},{12,8},{1,5},{13,9},{2,6},{14,10},{3,7},{15,11},{16,20},{28,... | collective-permute-start | bytes 393224 | tf_op jit(solution)/shard_map/ppermute | solution.py:172
  12.4 2.8 %collective-permute-start.1 = (bf16[32,2048]{1,0:T(8,128)(2,1)S(1)}, bf16[32,2048]{1,0:T(8,128)(2,1)S(1)}, u32[]{:S(2)}, u32[]{:S(2)}) collective-permute-start(bf16[32,2048]{1,0:T(8,128)(2,1)S(1)} %half_both.1), channel_id=1, source_target_pairs={{4,8},{8,4},{5,9},{9,5},{6,10},{10,6},{7,11},{11,7},{20,24},{24,20... | collective-permute-start | bytes 393224 | tf_op jit(solution)/shard_map/ppermute | solution.py:171
  15.3 9.8 %collective-permute-start.5 = (bf16[32,2048]{1,0:T(8,128)(2,1)S(1)}, bf16[32,2048]{1,0:T(8,128)(2,1)S(1)}, u32[]{:S(2)}, u32[]{:S(2)}) collective-permute-start(bf16[32,2048]{1,0:T(8,128)(2,1)S(1)} %add_convert_fusion.sum_ref), channel_id=1, source_target_pairs={{4,12},{8,0},{5,13},{9,1},{6,14},{10,2},{7,15},{11,3},{20,28},{24,... | collective-permute-start | bytes 393224 | tf_op jit(solution)/shard_map/ppermute | solution.py:178
  16.6 11.2 %collective-permute-start.4 = (bf16[32,2048]{1,0:T(8,128)(2,1)S(1)}, bf16[32,2048]{1,0:T(8,128)(2,1)S(1)}, u32[]{:S(2)}, u32[]{:S(2)}) collective-permute-start(bf16[32,2048]{1,0:T(8,128)(2,1)S(1)} %add_convert_fusion.sum_ref), channel_id=1, source_target_pairs={{4,0},{8,12},{5,1},{9,13},{6,2},{10,14},{7,3},{11,15},{20,16},{24,... | collective-permute-start | bytes 393224 | tf_op jit(solution)/shard_map/ppermute | solution.py:179
  17.9 9.9 %collective-permute-start.3 = (bf16[32,2048]{1,0:T(8,128)(2,1)S(1)}, bf16[32,2048]{1,0:T(8,128)(2,1)S(1)}, u32[]{:S(2)}, u32[]{:S(2)}) collective-permute-start(bf16[32,2048]{1,0:T(8,128)(2,1)S(1)} %add_convert_fusion.sum_ref), channel_id=1, source_target_pairs={{4,8},{8,4},{5,9},{9,5},{6,10},{10,6},{7,11},{11,7},{20,24},{24,20... | collective-permute-start | bytes 393224 | tf_op jit(solution)/shard_map/ppermute | solution.py:180
  28.5 1.2 %collective-permute-start.6 = (f32[16,256]{1,0:T(8,128)S(1)}, f32[16,256]{1,0:T(8,128)S(1)}, u32[]{:S(2)}, u32[]{:S(2)}) collective-permute-start(f32[16,256]{1,0:T(8,128)S(1)} %get-tuple-element.10), channel_id=1, source_target_pairs={{0,2},{2,0},{1,3},{3,1},{4,6},{6,4},{5,7},{7,5},{8,10},{10,8},{9,1... | collective-permute-start | bytes 49160 | tf_op jit(solution)/shard_map/ppermute | solution.py:160
  29.8 3.7 %collective-permute-start.7 = (f32[8,256]{1,0:T(8,128)S(1)}, f32[8,256]{1,0:T(8,128)S(1)}, u32[]{:S(2)}, u32[]{:S(2)}) collective-permute-start(f32[8,256]{1,0:T(8,128)S(1)} %get-tuple-element.12), channel_id=1, source_target_pairs={{0,1},{1,0},{2,3},{3,2},{4,5},{5,4},{6,7},{7,6},{8,9},{9,8},{10,11... | collective-permute-start | bytes 24584 | tf_op jit(solution)/shard_map/ppermute | solution.py:160

commit v2 on v0

v2 whole, which is shorter than its diff:
```python
import functools

import jax
import jax.numpy as jnp
from jax import lax
from jax.experimental import pallas as pl
from jax.experimental.pallas import tpu as pltpu
from jax.sharding import PartitionSpec as P

VMEM = pl.BlockSpec(memory_space=pltpu.VMEM)
ANY = pl.BlockSpec(memory_space=pl.ANY)
MIB = 2**20


def project_kernel(n, steps, chunks, test_ref, inverse_ref, *rest):
    outs, (test_buf, buf, total, test_sem, sems) = rest[: len(steps)], rest[len(steps) :]
    me = lax.axis_index("dp")
    rows = buf.shape[1]
    width = outs[0].shape[1]
    test_copy = pltpu.make_async_copy(test_ref.at[0], test_buf, test_sem)
    test_copy.start()
    starts = [pl.multiple_of(lax.bitwise_xor(me, step) * width, width) for step in steps]
    copies = [
        [
            pltpu.make_async_copy(
                inverse_ref.at[0, pl.ds(c * rows, rows), pl.ds(start, width)],
                buf.at[c, :, pl.ds(i * width, width)],
                sems.at[c, i],
            )
            for i, start in enumerate(starts)
        ]
        for c in range(chunks)
    ]
    for group in copies:
        for copy in group:
            copy.start()
    test_copy.wait()
    for c in range(chunks):
        for copy in copies[c]:
            copy.wait()
        term = jnp.dot(test_buf[:, c * rows : (c + 1) * rows], buf[c], preferred_element_type=jnp.float32)
        if c:
            term = total[...] + term
        if c < chunks - 1:
            total[...] = term
        else:
            for i, out in enumerate(outs):
                out[...] = term[:, i * width : (i + 1) * width].astype(out.dtype)


def project(n, steps, out_dtype, test, inverse):
    tests, depth = test.shape[1:]
    width = inverse.shape[2] // n
    rows = min(depth, 256)
    chunks = depth // rows
    wide = width * len(steps)
    return pl.pallas_call(
        functools.partial(project_kernel, n, steps, chunks),
        in_specs=[ANY, ANY],
        out_specs=[VMEM] * len(steps),
        out_shape=[jax.ShapeDtypeStruct((tests, width), out_dtype)] * len(steps),
        scratch_shapes=[
            pltpu.VMEM((tests, depth), test.dtype),
            pltpu.VMEM((chunks, rows, wide), inverse.dtype),
            pltpu.VMEM((tests, wide), jnp.float32),
            pltpu.SemaphoreType.DMA,
            pltpu.SemaphoreType.DMA((chunks, len(steps))),
        ],
        compiler_params=pltpu.CompilerParams(vmem_limit_bytes=52 * MIB),
        cost_estimate=pl.CostEstimate(
            flops=2 * tests * depth * wide, bytes_accessed=2 * depth * wide, transcendentals=0
        ),
        name="project",
    )(test, inverse)


def score_kernel(steps, parts, axes, *refs):
    count = len(steps)
    blocks, train_ref, weight_ref, outs, raw = refs[:count], refs[count], refs[count + 1], refs[count + 2 : -1], refs[-1]
    me = lax.axis_index("dp")
    width = blocks[0].shape[1]
    contract = (((1,), (1,)), ((), ()))
    value = None
    for step, block in zip(steps, blocks):
        columns = pl.ds(pl.multiple_of(lax.bitwise_xor(me, step) * width, width), width)
        term = lax.dot_general(block[...], train_ref[0, :, columns], contract, preferred_element_type=jnp.float32)
        value = term if value is None else value + term
    raw[...] = value * weight_ref[...]
    place = lax.axis_index(axes[0]) * (parts // lax.axis_size(axes[0])) + lax.axis_index(axes[1])
    rows = outs[0].shape[0]
    for step, out in enumerate(outs):
        out[...] = raw[pl.ds(pl.multiple_of(lax.bitwise_xor(place, step) * rows, rows), rows), :]


def score(n, parts, axes, blocks, train, weight):
    tests, width = blocks[0].shape
    columns = train.shape[1]
    return pl.pallas_call(
        functools.partial(score_kernel, range(n), parts, axes),
        in_specs=[VMEM] * (n + 2),
        out_specs=[VMEM] * parts,
        out_shape=[jax.ShapeDtypeStruct((tests // parts, columns), jnp.float32)] * parts,
        scratch_shapes=[pltpu.VMEM((tests, columns), jnp.float32)],
        compiler_params=pltpu.CompilerParams(vmem_limit_bytes=16 * MIB),
        cost_estimate=pl.CostEstimate(
            flops=2 * n * tests * columns * width, bytes_accessed=2 * n * columns * width, transcendentals=0
        ),
        name="score",
    )(*blocks, train, weight)


def swap(x, axes, n, step):
    return lax.ppermute(x, axes, [(i, i ^ step) for i in range(n)])


def line_shards(n, parts, axes, test_feat, kernel_inverse, train_feat, residual_weight):
    order = (3, 2, 1)
    away = project(n, order, jnp.bfloat16, test_feat, kernel_inverse)
    terms = [swap(block, "dp", n, step) for step, block in zip(order, away)]
    (own,) = project(n, (0,), jnp.float32, test_feat, kernel_inverse)
    total = own
    for term in terms:
        total = total + term
    total = total.astype(jnp.bfloat16)
    blocks = [total] + [swap(total, "dp", n, step) for step in range(1, n)]
    rows = score(n, parts, axes, blocks, train_feat, residual_weight)
    result = rows[0]
    for step in range(1, parts):
        result = result + swap(rows[step], axes, parts, step)
    return result


def general_shards(test_feat, kernel_inverse, train_feat, residual_weight):
    partial_sum = jnp.dot(test_feat[0], kernel_inverse[0], preferred_element_type=jnp.float32)
    projected = lax.psum(partial_sum, "dp").astype(jnp.bfloat16)
    raw = jnp.einsum("tf,nf->tn", projected, train_feat[0], preferred_element_type=jnp.float32)
    totals = raw * residual_weight[0][None, :]
    return lax.psum_scatter(totals, ("feat", "ens"), scatter_dimension=0, tiled=True)


def solution(mesh):
    in_specs = (
        P("ens", "groups", "dp"),
        P("ens", "dp", "feat"),
        P("ens", "dp", "feat"),
        P("ens", "dp"),
    )
    out_specs = P(("groups", "feat", "ens"), "dp")
    line, axes = mesh.shape["dp"], ("feat", "ens")
    parts = mesh.shape["feat"] * mesh.shape["ens"]
    if line == 4 and parts == 4:
        body = functools.partial(line_shards, line, parts, axes)
    else:
        body = general_shards
    return jax.shard_map(body, mesh=mesh, in_specs=in_specs, out_specs=out_specs, check_vma=False)
```

time: 74 us -> 32.8 us (0.44)
  blocking collectives: 32.1 us -> 0 us
  between operations: 13.4 us -> 0.05 us
  starting transfers between devices: 0.01 us -> 12.4 us
  matrix products: 10.3 us -> 0 us
  Pallas kernels: 0 us -> 8.67 us
  waiting for transfers between devices: 18 us -> 9.76 us
  local copies, waits for them, and re-layouts: 0.01 us -> 1.06 us
    psum x1 -> x0, blocking collectives: 32.1 us -> none  [shards(): projected = lax.psum(partial_sum, 'dp').astype(jnp.bfloat16)]
    reduce_scatter x1 -> x0, waiting for transfers between devices: 18 us -> none  [shards(): lax.psum_scatter(totals, ('feat', 'ens'), scatter_dimension=0, tiled=True)]
    ppermute x0 -> x9, starting transfers between devices: none -> 12.4 us  [swap(): return lax.ppermute(x, axes, [(i, i ^ step) for i in range(n)])]
    dot_general x2 -> x0, matrix products: 10.3 us -> none  [the longest x1 8.96 us: shards(): jnp.dot(test_local, inverse_local, preferred_element_type=jnp.float32)]
    ppermute x0 -> x9, waiting for transfers between devices: none -> 9.76 us  [swap(): return lax.ppermute(x, axes, [(i, i ^ step) for i in range(n)])]
    pallas_call x0 -> x3, Pallas kernels: none -> 8.67 us  [the longest x2 7.94 us: project(): pl.pallas_call(functools.partial(project_kernel, n, steps, chunks), in_sp...]
    unnamed x4 -> x6, local copies, waits for them, and re-layouts: 0.01 us -> 1.06 us
  transfers between devices with their start and end apart: 1 -> 9, of which waited for: 1 -> 6; matrix products, arithmetic and copies ran while one was open for 0% -> 0% of each run, Pallas kernels for 0% -> 8%
where the time goes in v2:
time: 32.8 us; the launch traced here: 32.6 us
  starting transfers between devices  12.4 us (38%)
  waiting for transfers between devices  9.76 us (30%)
  Pallas kernels  8.67 us (26%)
  local copies, waits for them, and re-layouts  1.06 us (3%)
  other arithmetic  0.64 us (2%)
    ppermute x9, starting transfers between devices, swap(): return lax.ppermute(x, axes, [(i, i ^ step) for i in range(n)])  12.4 us
    ppermute x9, waiting for transfers between devices, swap(): return lax.ppermute(x, axes, [(i, i ^ step) for i in range(n)])  9.76 us
    pallas_call x2, Pallas kernels, project(): pl.pallas_call(functools.partial(project_kernel, n, steps, chunks), in_sp...  7.94 us
    unnamed x6, local copies, waits for them, and re-layouts  1.06 us
    pallas_call x1, Pallas kernels, score(): pl.pallas_call(functools.partial(score_kernel, range(n), parts, axes), in...  0.73 us
  transfers between devices with their start and end apart: 9, of which 6 were waited for; matrix products, arithmetic and copies ran while one was open for 0% of the time, Pallas kernels for 8%

profile of v2, /device:TPU:0, one launch (start us, length us, event | category | flops | bytes accessed | tf_op | source)
XLA Modules:
  0.0 32.6 jit_solution(10771073360140682098)
XLA Ops:
  0.0 1.1 %copy-done.1 = bf16[1,32,2048]{2,1,0:T(8,128)(2,1)S(1)} copy-done((bf16[1,32,2048]{2,1,0:T(8,128)(2,1)S(1)}, bf16[1,32,2048]{2,1,0:T(8,128)(2,1)}, u32[]{:S(2)}) %copy-start.1) | copy-done | bytes 131096
  1.1 5.4 %project.3 = (bf16[32,1024]{1,0:T(8,128)(2,1)S(1)}, bf16[32,1024]{1,0:T(8,128)(2,1)S(1)}, bf16[32,1024]{1,0:T(8,128)(2,1)S(1)}) custom-call(bf16[1,32,2048]{2,1,0:T(8,128)(2,1)S(1)} %copy-done.1, bf16[1,2048,4096]{2,1,0:T(8,128)(2,1)} %inverse_ref.3), custom_call_target="tpu_custom_call" | custom-call | flops 402653184 | bytes 12582912 | tf_op jit(solution)/shard_map/project/pallas_call | solution.py:57
  6.4 5.1 %collective-permute-start = (bf16[32,1024]{1,0:T(8,128)(2,1)S(1)}, bf16[32,1024]{1,0:T(8,128)(2,1)S(1)}, u32[]{:S(2)}, u32[]{:S(2)}) collective-permute-start(bf16[32,1024]{1,0:T(8,128)(2,1)S(1)} %get-tuple-element.12), channel_id=1, source_target_pairs={{0,12},{4,8},{8,4},{12,0},{1,13},{5,9},{9,5},{13,1},{2,14},{6,10},... | collective-permute-start | bytes 196616 | tf_op jit(solution)/shard_map/ppermute | solution.py:113
  11.5 0.0 collective-permute-start.1
  11.5 0.6 %collective-permute-start.2 = (bf16[32,1024]{1,0:T(8,128)(2,1)S(1)}, bf16[32,1024]{1,0:T(8,128)(2,1)S(1)}, u32[]{:S(2)}, u32[]{:S(2)}) collective-permute-start(bf16[32,1024]{1,0:T(8,128)(2,1)S(1)} %get-tuple-element.14), channel_id=1, source_target_pairs={{0,4},{4,0},{8,12},{12,8},{1,5},{5,1},{9,13},{13,9},{2,6},{6,2},{1... | collective-permute-start | bytes 196616 | tf_op jit(solution)/shard_map/ppermute | solution.py:113
  12.2 2.6 %project.2 = f32[32,1024]{1,0:T(8,128)S(1)} custom-call(bf16[1,32,2048]{2,1,0:T(8,128)(2,1)S(1)} %copy-done.1, bf16[1,2048,4096]{2,1,0:T(8,128)(2,1)} %inverse_ref.3), custom_call_target="tpu_custom_call" | custom-call | flops 134217728 | bytes 4194304 | tf_op jit(solution)/shard_map/project/pallas_call | solution.py:57
  14.8 0.0 collective-permute-done
  14.8 2.4 %collective-permute-done.1 = bf16[32,1024]{1,0:T(8,128)(2,1)S(1)} collective-permute-done((bf16[32,1024]{1,0:T(8,128)(2,1)S(1)}, bf16[32,1024]{1,0:T(8,128)(2,1)S(1)}, u32[]{:S(2)}, u32[]{:S(2)}) %collective-permute-start.1) | collective-permute-done | bytes 65568 | tf_op jit(solution)/shard_map/ppermute | solution.py:113
  17.1 0.0 collective-permute-done.2
  17.2 1.1 %collective-permute-start.3 = (bf16[32,1024]{1,0:T(8,128)(2,1)S(1)}, bf16[32,1024]{1,0:T(8,128)(2,1)S(1)}, u32[]{:S(2)}, u32[]{:S(2)}) collective-permute-start(bf16[32,1024]{1,0:T(8,128)(2,1)S(1)} %add_convert_fusion.refs_0_), channel_id=1, source_target_pairs={{0,4},{4,0},{8,12},{12,8},{1,5},{5,1},{9,13},{13,9},{2,6},{6,2},{1... | collective-permute-start | bytes 196616 | tf_op jit(solution)/shard_map/ppermute | solution.py:113
  18.3 2.2 %collective-permute-start.4 = (bf16[32,1024]{1,0:T(8,128)(2,1)S(1)}, bf16[32,1024]{1,0:T(8,128)(2,1)S(1)}, u32[]{:S(2)}, u32[]{:S(2)}) collective-permute-start(bf16[32,1024]{1,0:T(8,128)(2,1)S(1)} %add_convert_fusion.refs_0_), channel_id=1, source_target_pairs={{0,8},{4,12},{8,0},{12,4},{1,9},{5,13},{9,1},{13,5},{2,10},{6,14},... | collective-permute-start | bytes 196616 | tf_op jit(solution)/shard_map/ppermute | solution.py:113
  20.5 1.1 %collective-permute-start.5 = (bf16[32,1024]{1,0:T(8,128)(2,1)S(1)}, bf16[32,1024]{1,0:T(8,128)(2,1)S(1)}, u32[]{:S(2)}, u32[]{:S(2)}) collective-permute-start(bf16[32,1024]{1,0:T(8,128)(2,1)S(1)} %add_convert_fusion.refs_0_), channel_id=1, source_target_pairs={{0,12},{4,8},{8,4},{12,0},{1,13},{5,9},{9,5},{13,1},{2,14},{6,10},... | collective-permute-start | bytes 196616 | tf_op jit(solution)/shard_map/ppermute | solution.py:113
  21.6 0.3 collective-permute-done.3.refs_1_
  21.9 3.0 %collective-permute-done.4.refs_2_ = bf16[32,1024]{1,0:T(8,128)(2,1)S(1)} collective-permute-done((bf16[32,1024]{1,0:T(8,128)(2,1)S(1)}, bf16[32,1024]{1,0:T(8,128)(2,1)S(1)}, u32[]{:S(2)}, u32[]{:S(2)}) %collective-permute-start.4) | collective-permute-done | bytes 65568 | tf_op jit(solution)/shard_map/ppermute | solution.py:113
  24.9 1.7 %collective-permute-done.5.refs_3_ = bf16[32,1024]{1,0:T(8,128)(2,1)S(1)} collective-permute-done((bf16[32,1024]{1,0:T(8,128)(2,1)S(1)}, bf16[32,1024]{1,0:T(8,128)(2,1)S(1)}, u32[]{:S(2)}, u32[]{:S(2)}) %collective-permute-start.5) | collective-permute-done | bytes 65568 | tf_op jit(solution)/shard_map/ppermute | solution.py:113
  26.6 0.0 copy-done.2
  26.6 0.7 %score.1 = (f32[8,256]{1,0:T(8,128)S(1)}, f32[8,256]{1,0:T(8,128)S(1)}, f32[8,256]{1,0:T(8,128)S(1)}, f32[8,256]{1,0:T(8,128)S(1)}) custom-call(bf16[32,1024]{1,0:T(8,128)(2,1)S(1)} %add_convert_fusion.refs_0_, bf16[32,1024]{1,0:T(8,128)(2,1)S(1)} %collective-permute-done.3.refs_1_, bf16[32,1024]{1,0:T(8,128)(2,1)S(1)} %collective-permute-done.4.refs_2_, ...), custom_call_target="tpu_custom_call" | custom-call | flops 67108864 | bytes 2097152 | tf_op jit(solution)/shard_map/score/pallas_call | solution.py:98
  27.4 1.6 %collective-permute-start.6 = (f32[8,256]{1,0:T(8,128)S(1)}, f32[8,256]{1,0:T(8,128)S(1)}, u32[]{:S(2)}, u32[]{:S(2)}) collective-permute-start(f32[8,256]{1,0:T(8,128)S(1)} %get-tuple-element.16), channel_id=1, source_target_pairs={{0,1},{1,0},{2,3},{3,2},{4,5},{5,4},{6,7},{7,6},{8,9},{9,8},{10,11... | collective-permute-start | bytes 24584 | tf_op jit(solution)/shard_map/ppermute | solution.py:113
  28.9 0.0 collective-permute-start.7
  28.9 0.6 %collective-permute-start.8 = (f32[8,256]{1,0:T(8,128)S(1)}, f32[8,256]{1,0:T(8,128)S(1)}, u32[]{:S(2)}, u32[]{:S(2)}) collective-permute-start(f32[8,256]{1,0:T(8,128)S(1)} %get-tuple-element.18), channel_id=1, source_target_pairs={{0,3},{1,2},{2,1},{3,0},{4,7},{5,6},{6,5},{7,4},{8,11},{9,10},{10,... | collective-permute-start | bytes 24584 | tf_op jit(solution)/shard_map/ppermute | solution.py:113
  29.6 1.5 %collective-permute-done.6 = f32[8,256]{1,0:T(8,128)S(1)} collective-permute-done((f32[8,256]{1,0:T(8,128)S(1)}, f32[8,256]{1,0:T(8,128)S(1)}, u32[]{:S(2)}, u32[]{:S(2)}) %collective-permute-start.6) | collective-permute-done | bytes 8224 | tf_op jit(solution)/shard_map/ppermute | solution.py:113
  31.1 0.0 collective-permute-done.7
  31.1 0.9 %collective-permute-done.8 = f32[8,256]{1,0:T(8,128)S(1)} collective-permute-done((f32[8,256]{1,0:T(8,128)S(1)}, f32[8,256]{1,0:T(8,128)S(1)}, u32[]{:S(2)}, u32[]{:S(2)}) %collective-permute-start.8) | collective-permute-done | bytes 8224 | tf_op jit(solution)/shard_map/ppermute | solution.py:113
  32.0 0.6 %add_add_fusion = f32[8,256]{1,0:T(8,128)} fusion(f32[8,256]{1,0:T(8,128)S(1)} %collective-permute-done.8, f32[8,256]{1,0:T(8,128)S(1)} %collective-permute-done.7, f32[8,256]{1,0:T(8,128)S(1)} %get-tuple-element.15, f32[8,256]{1,0:T(8,128)S(1)} %collective-permute-done.6), kind=kLoop, calls=%fused_computation.1 | loop fusion | flops 6144 | bytes 40960 | tf_op jit(solution)/shard_map/add | solution.py:129
  (5 shorter events, 0.0 us)
Async XLA Ops:
  0.0 26.6 %copy-start = (bf16[1,256,4096]{2,1,0:T(8,128)(2,1)S(1)}, bf16[1,256,4096]{2,1,0:T(8,128)(2,1)}, u32[]{:S(2)}) copy-start(bf16[1,256,4096]{2,1,0:T(8,128)(2,1)} %refs_4_.1) | copy-start | bytes 6291460
  0.0 1.1 %copy-start.1 = (bf16[1,32,2048]{2,1,0:T(8,128)(2,1)S(1)}, bf16[1,32,2048]{2,1,0:T(8,128)(2,1)}, u32[]{:S(2)}) copy-start(bf16[1,32,2048]{2,1,0:T(8,128)(2,1)} %test_ref.3) | copy-start | bytes 393220
  1.1 25.6 %copy-start.2 = (f32[1,256]{1,0:T(1,128)S(1)}, f32[1,256]{1,0:T(1,128)}, u32[]{:S(2)}) copy-start(f32[1,256]{1,0:T(1,128)} %refs_5_.1) | copy-start | bytes 3076
  6.4 8.3 %collective-permute-start = (bf16[32,1024]{1,0:T(8,128)(2,1)S(1)}, bf16[32,1024]{1,0:T(8,128)(2,1)S(1)}, u32[]{:S(2)}, u32[]{:S(2)}) collective-permute-start(bf16[32,1024]{1,0:T(8,128)(2,1)S(1)} %get-tuple-element.12), channel_id=1, source_target_pairs={{0,12},{4,8},{8,4},{12,0},{1,13},{5,9},{9,5},{13,1},{2,14},{6,10},... | collective-permute-start | bytes 196616 | tf_op jit(solution)/shard_map/ppermute | solution.py:113
  11.5 5.6 %collective-permute-start.1 = (bf16[32,1024]{1,0:T(8,128)(2,1)S(1)}, bf16[32,1024]{1,0:T(8,128)(2,1)S(1)}, u32[]{:S(2)}, u32[]{:S(2)}) collective-permute-start(bf16[32,1024]{1,0:T(8,128)(2,1)S(1)} %get-tuple-element.13), channel_id=1, source_target_pairs={{0,8},{4,12},{8,0},{12,4},{1,9},{5,13},{9,1},{13,5},{2,10},{6,14},... | collective-permute-start | bytes 196616 | tf_op jit(solution)/shard_map/ppermute | solution.py:113
  11.5 5.6 %collective-permute-start.2 = (bf16[32,1024]{1,0:T(8,128)(2,1)S(1)}, bf16[32,1024]{1,0:T(8,128)(2,1)S(1)}, u32[]{:S(2)}, u32[]{:S(2)}) collective-permute-start(bf16[32,1024]{1,0:T(8,128)(2,1)S(1)} %get-tuple-element.14), channel_id=1, source_target_pairs={{0,4},{4,0},{8,12},{12,8},{1,5},{5,1},{9,13},{13,9},{2,6},{6,2},{1... | collective-permute-start | bytes 196616 | tf_op jit(solution)/shard_map/ppermute | solution.py:113
  17.2 4.7 %collective-permute-start.3 = (bf16[32,1024]{1,0:T(8,128)(2,1)S(1)}, bf16[32,1024]{1,0:T(8,128)(2,1)S(1)}, u32[]{:S(2)}, u32[]{:S(2)}) collective-permute-start(bf16[32,1024]{1,0:T(8,128)(2,1)S(1)} %add_convert_fusion.refs_0_), channel_id=1, source_target_pairs={{0,4},{4,0},{8,12},{12,8},{1,5},{5,1},{9,13},{13,9},{2,6},{6,2},{1... | collective-permute-start | bytes 196616 | tf_op jit(solution)/shard_map/ppermute | solution.py:113
  18.3 6.6 %collective-permute-start.4 = (bf16[32,1024]{1,0:T(8,128)(2,1)S(1)}, bf16[32,1024]{1,0:T(8,128)(2,1)S(1)}, u32[]{:S(2)}, u32[]{:S(2)}) collective-permute-start(bf16[32,1024]{1,0:T(8,128)(2,1)S(1)} %add_convert_fusion.refs_0_), channel_id=1, source_target_pairs={{0,8},{4,12},{8,0},{12,4},{1,9},{5,13},{9,1},{13,5},{2,10},{6,14},... | collective-permute-start | bytes 196616 | tf_op jit(solution)/shard_map/ppermute | solution.py:113
  20.5 6.1 %collective-permute-start.5 = (bf16[32,1024]{1,0:T(8,128)(2,1)S(1)}, bf16[32,1024]{1,0:T(8,128)(2,1)S(1)}, u32[]{:S(2)}, u32[]{:S(2)}) collective-permute-start(bf16[32,1024]{1,0:T(8,128)(2,1)S(1)} %add_convert_fusion.refs_0_), channel_id=1, source_target_pairs={{0,12},{4,8},{8,4},{12,0},{1,13},{5,9},{9,5},{13,1},{2,14},{6,10},... | collective-permute-start | bytes 196616 | tf_op jit(solution)/shard_map/ppermute | solution.py:113
  27.4 3.7 %collective-permute-start.6 = (f32[8,256]{1,0:T(8,128)S(1)}, f32[8,256]{1,0:T(8,128)S(1)}, u32[]{:S(2)}, u32[]{:S(2)}) collective-permute-start(f32[8,256]{1,0:T(8,128)S(1)} %get-tuple-element.16), channel_id=1, source_target_pairs={{0,1},{1,0},{2,3},{3,2},{4,5},{5,4},{6,7},{7,6},{8,9},{9,8},{10,11... | collective-permute-start | bytes 24584 | tf_op jit(solution)/shard_map/ppermute | solution.py:113
  28.9 2.2 %collective-permute-start.7 = (f32[8,256]{1,0:T(8,128)S(1)}, f32[8,256]{1,0:T(8,128)S(1)}, u32[]{:S(2)}, u32[]{:S(2)}) collective-permute-start(f32[8,256]{1,0:T(8,128)S(1)} %get-tuple-element.17), channel_id=1, source_target_pairs={{0,2},{1,3},{2,0},{3,1},{4,6},{5,7},{6,4},{7,5},{8,10},{9,11},{10,... | collective-permute-start | bytes 24584 | tf_op jit(solution)/shard_map/ppermute | solution.py:113
  28.9 3.1 %collective-permute-start.8 = (f32[8,256]{1,0:T(8,128)S(1)}, f32[8,256]{1,0:T(8,128)S(1)}, u32[]{:S(2)}, u32[]{:S(2)}) collective-permute-start(f32[8,256]{1,0:T(8,128)S(1)} %get-tuple-element.18), channel_id=1, source_target_pairs={{0,3},{1,2},{2,1},{3,0},{4,7},{5,6},{6,5},{7,4},{8,11},{9,10},{10,... | collective-permute-start | bytes 24584 | tf_op jit(solution)/shard_map/ppermute | solution.py:113

commit v3 on v2

--- a/solution.py
+++ b/solution.py
@@ -13,28 +13,23 @@
 
 
 def project_kernel(n, steps, chunks, test_ref, inverse_ref, *rest):
-    outs, (test_buf, buf, total, test_sem, sems) = rest[: len(steps)], rest[len(steps) :]
+    outs, (test_buf, buf, total, test_sems, sems) = rest[: len(steps)], rest[len(steps) :]
     me = lax.axis_index("dp")
     rows = buf.shape[1]
     width = outs[0].shape[1]
-    test_copy = pltpu.make_async_copy(test_ref.at[0], test_buf, test_sem)
-    test_copy.start()
     starts = [pl.multiple_of(lax.bitwise_xor(me, step) * width, width) for step in steps]
-    copies = [
-        [
-            pltpu.make_async_copy(
-                inverse_ref.at[0, pl.ds(c * rows, rows), pl.ds(start, width)],
-                buf.at[c, :, pl.ds(i * width, width)],
-                sems.at[c, i],
+    copies = []
+    for c in range(chunks):
+        part = pl.ds(c * rows, rows)
+        test_copy = pltpu.make_async_copy(test_ref.at[0, :, part], test_buf.at[:, part], test_sems.at[c])
+        test_copy.start()
+        copies.append([test_copy])
+        for i, start in enumerate(starts):
+            copy = pltpu.make_async_copy(
+                inverse_ref.at[0, part, pl.ds(start, width)], buf.at[c, :, pl.ds(i * width, width)], sems.at[c, i]
             )
-            for i, start in enumerate(starts)
-        ]
-        for c in range(chunks)
-    ]
-    for group in copies:
-        for copy in group:
-            copy.start()
-    test_copy.wait()
+            copy.start(priority=1)
+            copies[c].append(copy)
     for c in range(chunks):
         for copy in copies[c]:
             copy.wait()
@@ -63,10 +58,10 @@
             pltpu.VMEM((tests, depth), test.dtype),
             pltpu.VMEM((chunks, rows, wide), inverse.dtype),
             pltpu.VMEM((tests, wide), jnp.float32),
-            pltpu.SemaphoreType.DMA,
+            pltpu.SemaphoreType.DMA((chunks,)),
             pltpu.SemaphoreType.DMA((chunks, len(steps))),
         ],
-        compiler_params=pltpu.CompilerParams(vmem_limit_bytes=52 * MIB),
+        compiler_params=pltpu.CompilerParams(vmem_limit_bytes=215 * MIB // 4),
         cost_estimate=pl.CostEstimate(
             flops=2 * tests * depth * wide, bytes_accessed=2 * depth * wide, transcendentals=0
         ),
@@ -76,7 +71,7 @@
 
 def score_kernel(steps, parts, axes, *refs):
     count = len(steps)
-    blocks, train_ref, weight_ref, outs, raw = refs[:count], refs[count], refs[count + 1], refs[count + 2 : -1], refs[-1]
+    blocks, train_ref, refs = refs[:count], refs[count], refs[count + 1 :]
     me = lax.axis_index("dp")
     width = blocks[0].shape[1]
     contract = (((1,), (1,)), ((), ()))
@@ -85,28 +80,34 @@
         columns = pl.ds(pl.multiple_of(lax.bitwise_xor(me, step) * width, width), width)
         term = lax.dot_general(block[...], train_ref[0, :, columns], contract, preferred_element_type=jnp.float32)
         value = term if value is None else value + term
-    raw[...] = value * weight_ref[...]
+    if not parts:
+        refs[0][...] = value
+        return
+    so_far, weight_ref, outs, raw = refs[0], refs[1], refs[2:-1], refs[-1]
+    raw[...] = (so_far[...] + value) * weight_ref[...]
     place = lax.axis_index(axes[0]) * (parts // lax.axis_size(axes[0])) + lax.axis_index(axes[1])
     rows = outs[0].shape[0]
     for step, out in enumerate(outs):
         out[...] = raw[pl.ds(pl.multiple_of(lax.bitwise_xor(place, step) * rows, rows), rows), :]
 
 
-def score(n, parts, axes, blocks, train, weight):
+def score(steps, parts, axes, blocks, train, *more):
     tests, width = blocks[0].shape
     columns = train.shape[1]
+    count = len(blocks)
+    out = [jax.ShapeDtypeStruct((tests // max(parts, 1), columns), jnp.float32)] * max(parts, 1)
     return pl.pallas_call(
-        functools.partial(score_kernel, range(n), parts, axes),
-        in_specs=[VMEM] * (n + 2),
-        out_specs=[VMEM] * parts,
-        out_shape=[jax.ShapeDtypeStruct((tests // parts, columns), jnp.float32)] * parts,
-        scratch_shapes=[pltpu.VMEM((tests, columns), jnp.float32)],
+        functools.partial(score_kernel, steps, parts, axes),
+        in_specs=[VMEM] * (count + 1 + len(more)),
+        out_specs=[VMEM] * len(out),
+        out_shape=out,
+        scratch_shapes=[pltpu.VMEM((tests, columns), jnp.float32)] * bool(parts),
         compiler_params=pltpu.CompilerParams(vmem_limit_bytes=16 * MIB),
         cost_estimate=pl.CostEstimate(
-            flops=2 * n * tests * columns * width, bytes_accessed=2 * n * columns * width, transcendentals=0
+            flops=2 * count * tests * columns * width, bytes_accessed=2 * count * columns * width, transcendentals=0
         ),
         name="score",
-    )(*blocks, train, weight)
+    )(*blocks, train, *more)
 
 
 def swap(x, axes, n, step):
@@ -116,16 +117,19 @@
 def line_shards(n, parts, axes, test_feat, kernel_inverse, train_feat, residual_weight):
     order = (3, 2, 1)
     away = project(n, order, jnp.bfloat16, test_feat, kernel_inverse)
-    terms = [swap(block, "dp", n, step) for step, block in zip(order, away)]
+    sent = {step: swap(block, "dp", n, step) for step, block in zip(order, away)}
     (own,) = project(n, (0,), jnp.float32, test_feat, kernel_inverse)
     total = own
-    for term in terms:
-        total = total + term
+    for step in (3, 1, 2):
+        total = total + sent[step]
     total = total.astype(jnp.bfloat16)
-    blocks = [total] + [swap(total, "dp", n, step) for step in range(1, n)]
-    rows = score(n, parts, axes, blocks, train_feat, residual_weight)
+    back = (3, 2, 1)
+    blocks = [total] + [swap(total, "dp", n, step) for step in back]
+    first = 2
+    (raw,) = score((0, *back)[:first], 0, axes, blocks[:first], train_feat)
+    rows = score((0, *back)[first:], parts, axes, blocks[first:], train_feat, raw, residual_weight)
     result = rows[0]
-    for step in range(1, parts):
+    for step in (3, 1, 2):
         result = result + swap(rows[step], axes, parts, step)
     return result
 

time: 32.8 us -> 29.3 us (0.89)
  waiting for transfers between devices: 9.76 us -> 7.46 us
  local copies, waits for them, and re-layouts: 1.06 us -> 0.01 us
    ppermute x9, waiting for transfers between devices: 9.76 us -> 7.46 us  [swap(): return lax.ppermute(x, axes, [(i, i ^ step) for i in range(n)])]
    unnamed x6 -> x4, local copies, waits for them, and re-layouts: 1.06 us -> 0.01 us
    pallas_call x1 -> x2, Pallas kernels: 0.73 us -> 0.83 us  [score(): pl.pallas_call(functools.partial(score_kernel, steps, parts, axes), in_sp...]
  transfers between devices with their start and end apart: 9 -> 9, of which waited for: 6 -> 6; matrix products, arithmetic and copies ran while one was open for 0% -> 0% of each run, Pallas kernels for 8% -> 10%
where the time goes in v3:
time: 29.3 us; the launch traced here: 29.2 us
  starting transfers between devices  12.1 us (41%)
  Pallas kernels  8.88 us (30%)
  waiting for transfers between devices  7.46 us (25%)
  other arithmetic  0.64 us (2%)
    ppermute x9, starting transfers between devices, swap(): return lax.ppermute(x, axes, [(i, i ^ step) for i in range(n)])  12.1 us
    pallas_call x2, Pallas kernels, project(): pl.pallas_call(functools.partial(project_kernel, n, steps, chunks), in_sp...  8.05 us
    ppermute x9, waiting for transfers between devices, swap(): return lax.ppermute(x, axes, [(i, i ^ step) for i in range(n)])  7.46 us
    pallas_call x2, Pallas kernels, score(): pl.pallas_call(functools.partial(score_kernel, steps, parts, axes), in_sp...  0.83 us
    add x1, other arithmetic, line_shards(): result = result + swap(rows[step], axes, parts, step)  0.6 us
  transfers between devices with their start and end apart: 9, of which 6 were waited for; matrix products, arithmetic and copies ran while one was open for 0% of the time, Pallas kernels for 10%

profile of v3, /device:TPU:0, one launch (start us, length us, event | category | flops | bytes accessed | tf_op | source)
XLA Modules:
  0.0 29.2 jit_solution(8440605828913549384)
XLA Ops:
  0.0 5.5 %project.3 = (bf16[32,1024]{1,0:T(8,128)(2,1)S(1)}, bf16[32,1024]{1,0:T(8,128)(2,1)S(1)}, bf16[32,1024]{1,0:T(8,128)(2,1)S(1)}) custom-call(bf16[1,32,2048]{2,1,0:T(8,128)(2,1)} %test_ref.3, bf16[1,2048,4096]{2,1,0:T(8,128)(2,1)} %inverse_ref.3), custom_call_target="tpu_custom_call" | custom-call | flops 402653184 | bytes 12582912 | tf_op jit(solution)/shard_map/project/pallas_call | solution.py:52
  5.5 5.1 %collective-permute-start = (bf16[32,1024]{1,0:T(8,128)(2,1)S(1)}, bf16[32,1024]{1,0:T(8,128)(2,1)S(1)}, u32[]{:S(2)}, u32[]{:S(2)}) collective-permute-start(bf16[32,1024]{1,0:T(8,128)(2,1)S(1)} %get-tuple-element.12), channel_id=1, source_target_pairs={{0,12},{4,8},{8,4},{12,0},{1,13},{5,9},{9,5},{13,1},{2,14},{6,10},... | collective-permute-start | bytes 196616 | tf_op jit(solution)/shard_map/ppermute | solution.py:114
  10.6 0.0 collective-permute-start.1
  10.6 0.6 %collective-permute-start.2 = (bf16[32,1024]{1,0:T(8,128)(2,1)S(1)}, bf16[32,1024]{1,0:T(8,128)(2,1)S(1)}, u32[]{:S(2)}, u32[]{:S(2)}) collective-permute-start(bf16[32,1024]{1,0:T(8,128)(2,1)S(1)} %get-tuple-element.14), channel_id=1, source_target_pairs={{0,8},{4,12},{8,0},{12,4},{1,9},{5,13},{9,1},{13,5},{2,10},{6,14},... | collective-permute-start | bytes 196616 | tf_op jit(solution)/shard_map/ppermute | solution.py:114
  11.2 2.6 %project.2 = f32[32,1024]{1,0:T(8,128)S(1)} custom-call(bf16[1,32,2048]{2,1,0:T(8,128)(2,1)} %test_ref.3, bf16[1,2048,4096]{2,1,0:T(8,128)(2,1)} %inverse_ref.3), custom_call_target="tpu_custom_call" | custom-call | flops 134217728 | bytes 4194304 | tf_op jit(solution)/shard_map/project/pallas_call | solution.py:52
  13.8 0.0 collective-permute-done
  13.8 1.4 %collective-permute-done.1 = bf16[32,1024]{1,0:T(8,128)(2,1)S(1)} collective-permute-done((bf16[32,1024]{1,0:T(8,128)(2,1)S(1)}, bf16[32,1024]{1,0:T(8,128)(2,1)S(1)}, u32[]{:S(2)}, u32[]{:S(2)}) %collective-permute-start.1) | collective-permute-done | bytes 65568 | tf_op jit(solution)/shard_map/ppermute | solution.py:114
  15.3 1.0 %collective-permute-done.2 = bf16[32,1024]{1,0:T(8,128)(2,1)S(1)} collective-permute-done((bf16[32,1024]{1,0:T(8,128)(2,1)S(1)}, bf16[32,1024]{1,0:T(8,128)(2,1)S(1)}, u32[]{:S(2)}, u32[]{:S(2)}) %collective-permute-start.2) | collective-permute-done | bytes 65568 | tf_op jit(solution)/shard_map/ppermute | solution.py:114
  16.3 2.2 %collective-permute-start.5 = (bf16[32,1024]{1,0:T(8,128)(2,1)S(1)}, bf16[32,1024]{1,0:T(8,128)(2,1)S(1)}, u32[]{:S(2)}, u32[]{:S(2)}) collective-permute-start(bf16[32,1024]{1,0:T(8,128)(2,1)S(1)} %add_convert_fusion.refs_0_), channel_id=1, source_target_pairs={{0,12},{4,8},{8,4},{12,0},{1,13},{5,9},{9,5},{13,1},{2,14},{6,10},... | collective-permute-start | bytes 196616 | tf_op jit(solution)/shard_map/ppermute | solution.py:114
  18.5 0.9 %collective-permute-start.3 = (bf16[32,1024]{1,0:T(8,128)(2,1)S(1)}, bf16[32,1024]{1,0:T(8,128)(2,1)S(1)}, u32[]{:S(2)}, u32[]{:S(2)}) collective-permute-start(bf16[32,1024]{1,0:T(8,128)(2,1)S(1)} %add_convert_fusion.refs_0_), channel_id=1, source_target_pairs={{0,8},{4,12},{8,0},{12,4},{1,9},{5,13},{9,1},{13,5},{2,10},{6,14},... | collective-permute-start | bytes 196616 | tf_op jit(solution)/shard_map/ppermute | solution.py:114
  19.4 1.4 %collective-permute-start.4 = (bf16[32,1024]{1,0:T(8,128)(2,1)S(1)}, bf16[32,1024]{1,0:T(8,128)(2,1)S(1)}, u32[]{:S(2)}, u32[]{:S(2)}) collective-permute-start(bf16[32,1024]{1,0:T(8,128)(2,1)S(1)} %add_convert_fusion.refs_0_), channel_id=1, source_target_pairs={{0,4},{4,0},{8,12},{12,8},{1,5},{5,1},{9,13},{13,9},{2,6},{6,2},{1... | collective-permute-start | bytes 196616 | tf_op jit(solution)/shard_map/ppermute | solution.py:114
  20.7 2.1 %collective-permute-done.5.refs_1_ = bf16[32,1024]{1,0:T(8,128)(2,1)S(1)} collective-permute-done((bf16[32,1024]{1,0:T(8,128)(2,1)S(1)}, bf16[32,1024]{1,0:T(8,128)(2,1)S(1)}, u32[]{:S(2)}, u32[]{:S(2)}) %collective-permute-start.5) | collective-permute-done | bytes 65568 | tf_op jit(solution)/shard_map/ppermute | solution.py:114
  22.8 0.0 copy-done
  22.8 0.4 %score.2.refs_3_ = f32[32,256]{1,0:T(8,128)S(1)} custom-call(bf16[32,1024]{1,0:T(8,128)(2,1)S(1)} %add_convert_fusion.refs_0_, bf16[32,1024]{1,0:T(8,128)(2,1)S(1)} %collective-permute-done.5.refs_1_, bf16[1,256,4096]{2,1,0:T(8,128)(2,1)S(1)} %copy-done), custom_call_target="tpu_custom_call" | custom-call | flops 33554432 | bytes 1048576 | tf_op jit(solution)/shard_map/score/pallas_call | solution.py:99
  23.2 1.1 %collective-permute-done.3.refs_0_ = bf16[32,1024]{1,0:T(8,128)(2,1)S(1)} collective-permute-done((bf16[32,1024]{1,0:T(8,128)(2,1)S(1)}, bf16[32,1024]{1,0:T(8,128)(2,1)S(1)}, u32[]{:S(2)}, u32[]{:S(2)}) %collective-permute-start.3) | collective-permute-done | bytes 65568 | tf_op jit(solution)/shard_map/ppermute | solution.py:114
  24.3 0.0 collective-permute-done.4.refs_1_
  24.3 0.4 %score.3 = (f32[8,256]{1,0:T(8,128)S(1)}, f32[8,256]{1,0:T(8,128)S(1)}, f32[8,256]{1,0:T(8,128)S(1)}, f32[8,256]{1,0:T(8,128)S(1)}) custom-call(bf16[32,1024]{1,0:T(8,128)(2,1)S(1)} %collective-permute-done.3.refs_0_, bf16[32,1024]{1,0:T(8,128)(2,1)S(1)} %collective-permute-done.4.refs_1_, bf16[1,256,4096]{2,1,0:T(8,128)(2,1)S(1)} %copy-done, ...), custom_call_target="tpu_custom_call" | custom-call | flops 33554432 | bytes 1048576 | tf_op jit(solution)/shard_map/score/pallas_call | solution.py:99
  24.8 0.1 collective-permute-start.6
  24.9 1.6 %collective-permute-start.7 = (f32[8,256]{1,0:T(8,128)S(1)}, f32[8,256]{1,0:T(8,128)S(1)}, u32[]{:S(2)}, u32[]{:S(2)}) collective-permute-start(f32[8,256]{1,0:T(8,128)S(1)} %get-tuple-element.17), channel_id=1, source_target_pairs={{0,1},{1,0},{2,3},{3,2},{4,5},{5,4},{6,7},{7,6},{8,9},{9,8},{10,11... | collective-permute-start | bytes 24584 | tf_op jit(solution)/shard_map/ppermute | solution.py:114
  26.5 0.2 collective-permute-start.8
  26.7 1.2 %collective-permute-done.6 = f32[8,256]{1,0:T(8,128)S(1)} collective-permute-done((f32[8,256]{1,0:T(8,128)S(1)}, f32[8,256]{1,0:T(8,128)S(1)}, u32[]{:S(2)}, u32[]{:S(2)}) %collective-permute-start.6) | collective-permute-done | bytes 8224 | tf_op jit(solution)/shard_map/ppermute | solution.py:114
  27.9 0.7 %collective-permute-done.7 = f32[8,256]{1,0:T(8,128)S(1)} collective-permute-done((f32[8,256]{1,0:T(8,128)S(1)}, f32[8,256]{1,0:T(8,128)S(1)}, u32[]{:S(2)}, u32[]{:S(2)}) %collective-permute-start.7) | collective-permute-done | bytes 8224 | tf_op jit(solution)/shard_map/ppermute | solution.py:114
  28.6 0.0 collective-permute-done.8
  28.6 0.6 %add_add_fusion = f32[8,256]{1,0:T(8,128)} fusion(f32[8,256]{1,0:T(8,128)S(1)} %collective-permute-done.8, f32[8,256]{1,0:T(8,128)S(1)} %collective-permute-done.7, f32[8,256]{1,0:T(8,128)S(1)} %get-tuple-element.15, f32[8,256]{1,0:T(8,128)S(1)} %collective-permute-done.6), kind=kLoop, calls=%fused_computation.1 | loop fusion | flops 6144 | bytes 40960 | tf_op jit(solution)/shard_map/add | solution.py:133
  (4 shorter events, 0.0 us)
Async XLA Ops:
  0.0 22.8 %copy-start = (bf16[1,256,4096]{2,1,0:T(8,128)(2,1)S(1)}, bf16[1,256,4096]{2,1,0:T(8,128)(2,1)}, u32[]{:S(2)}) copy-start(bf16[1,256,4096]{2,1,0:T(8,128)(2,1)} %refs_2_.3) | copy-start | bytes 6291460
  0.0 24.3 %copy-start.1 = (f32[1,256]{1,0:T(1,128)S(1)}, f32[1,256]{1,0:T(1,128)}, u32[]{:S(2)}) copy-start(f32[1,256]{1,0:T(1,128)} %refs_4_.1) | copy-start | bytes 3076
  5.5 8.4 %collective-permute-start = (bf16[32,1024]{1,0:T(8,128)(2,1)S(1)}, bf16[32,1024]{1,0:T(8,128)(2,1)S(1)}, u32[]{:S(2)}, u32[]{:S(2)}) collective-permute-start(bf16[32,1024]{1,0:T(8,128)(2,1)S(1)} %get-tuple-element.12), channel_id=1, source_target_pairs={{0,12},{4,8},{8,4},{12,0},{1,13},{5,9},{9,5},{13,1},{2,14},{6,10},... | collective-permute-start | bytes 196616 | tf_op jit(solution)/shard_map/ppermute | solution.py:114
  10.6 4.7 %collective-permute-start.1 = (bf16[32,1024]{1,0:T(8,128)(2,1)S(1)}, bf16[32,1024]{1,0:T(8,128)(2,1)S(1)}, u32[]{:S(2)}, u32[]{:S(2)}) collective-permute-start(bf16[32,1024]{1,0:T(8,128)(2,1)S(1)} %get-tuple-element.13), channel_id=1, source_target_pairs={{0,4},{4,0},{8,12},{12,8},{1,5},{5,1},{9,13},{13,9},{2,6},{6,2},{1... | collective-permute-start | bytes 196616 | tf_op jit(solution)/shard_map/ppermute | solution.py:114
  10.6 5.6 %collective-permute-start.2 = (bf16[32,1024]{1,0:T(8,128)(2,1)S(1)}, bf16[32,1024]{1,0:T(8,128)(2,1)S(1)}, u32[]{:S(2)}, u32[]{:S(2)}) collective-permute-start(bf16[32,1024]{1,0:T(8,128)(2,1)S(1)} %get-tuple-element.14), channel_id=1, source_target_pairs={{0,8},{4,12},{8,0},{12,4},{1,9},{5,13},{9,1},{13,5},{2,10},{6,14},... | collective-permute-start | bytes 196616 | tf_op jit(solution)/shard_map/ppermute | solution.py:114
  16.3 6.5 %collective-permute-start.5 = (bf16[32,1024]{1,0:T(8,128)(2,1)S(1)}, bf16[32,1024]{1,0:T(8,128)(2,1)S(1)}, u32[]{:S(2)}, u32[]{:S(2)}) collective-permute-start(bf16[32,1024]{1,0:T(8,128)(2,1)S(1)} %add_convert_fusion.refs_0_), channel_id=1, source_target_pairs={{0,12},{4,8},{8,4},{12,0},{1,13},{5,9},{9,5},{13,1},{2,14},{6,10},... | collective-permute-start | bytes 196616 | tf_op jit(solution)/shard_map/ppermute | solution.py:114
  18.5 5.8 %collective-permute-start.3 = (bf16[32,1024]{1,0:T(8,128)(2,1)S(1)}, bf16[32,1024]{1,0:T(8,128)(2,1)S(1)}, u32[]{:S(2)}, u32[]{:S(2)}) collective-permute-start(bf16[32,1024]{1,0:T(8,128)(2,1)S(1)} %add_convert_fusion.refs_0_), channel_id=1, source_target_pairs={{0,8},{4,12},{8,0},{12,4},{1,9},{5,13},{9,1},{13,5},{2,10},{6,14},... | collective-permute-start | bytes 196616 | tf_op jit(solution)/shard_map/ppermute | solution.py:114
  19.4 5.0 %collective-permute-start.4 = (bf16[32,1024]{1,0:T(8,128)(2,1)S(1)}, bf16[32,1024]{1,0:T(8,128)(2,1)S(1)}, u32[]{:S(2)}, u32[]{:S(2)}) collective-permute-start(bf16[32,1024]{1,0:T(8,128)(2,1)S(1)} %add_convert_fusion.refs_0_), channel_id=1, source_target_pairs={{0,4},{4,0},{8,12},{12,8},{1,5},{5,1},{9,13},{13,9},{2,6},{6,2},{1... | collective-permute-start | bytes 196616 | tf_op jit(solution)/shard_map/ppermute | solution.py:114
  24.8 3.1 %collective-permute-start.6 = (f32[8,256]{1,0:T(8,128)S(1)}, f32[8,256]{1,0:T(8,128)S(1)}, u32[]{:S(2)}, u32[]{:S(2)}) collective-permute-start(f32[8,256]{1,0:T(8,128)S(1)} %get-tuple-element.16), channel_id=1, source_target_pairs={{0,3},{1,2},{2,1},{3,0},{4,7},{5,6},{6,5},{7,4},{8,11},{9,10},{10,... | collective-permute-start | bytes 24584 | tf_op jit(solution)/shard_map/ppermute | solution.py:114
  24.9 3.7 %collective-permute-start.7 = (f32[8,256]{1,0:T(8,128)S(1)}, f32[8,256]{1,0:T(8,128)S(1)}, u32[]{:S(2)}, u32[]{:S(2)}) collective-permute-start(f32[8,256]{1,0:T(8,128)S(1)} %get-tuple-element.17), channel_id=1, source_target_pairs={{0,1},{1,0},{2,3},{3,2},{4,5},{5,4},{6,7},{7,6},{8,9},{9,8},{10,11... | collective-permute-start | bytes 24584 | tf_op jit(solution)/shard_map/ppermute | solution.py:114
  26.5 2.1 %collective-permute-start.8 = (f32[8,256]{1,0:T(8,128)S(1)}, f32[8,256]{1,0:T(8,128)S(1)}, u32[]{:S(2)}, u32[]{:S(2)}) collective-permute-start(f32[8,256]{1,0:T(8,128)S(1)} %get-tuple-element.18), channel_id=1, source_target_pairs={{0,2},{1,3},{2,0},{3,1},{4,6},{5,7},{6,4},{7,5},{8,10},{9,11},{10,... | collective-permute-start | bytes 24584 | tf_op jit(solution)/shard_map/ppermute | solution.py:114

commit v4 on v3

v4 whole, which is shorter than its diff:
```python
import functools

import jax
import jax.numpy as jnp
from jax import lax
from jax.experimental import pallas as pl
from jax.experimental.pallas import tpu as pltpu
from jax.sharding import PartitionSpec as P

VMEM = pl.BlockSpec(memory_space=pltpu.VMEM)
ANY = pl.BlockSpec(memory_space=pl.ANY)
MIB = 2**20
LANES = 128
SHORT_LINE = 4


def pick(table, z):
    value = table[0]
    for i, entry in enumerate(table[1:], 1):
        value = jnp.where(z == i, entry, value)
    return value


def sources(table):
    return tuple(table.index(i) for i in range(len(table)))


def plain_ring(n, step):
    return tuple((z + step) % n for z in range(n))


def folded_ring(n, step):
    ring = (0, *range(1, n, 2), *range(n - 2, 0, -2))
    return tuple(ring[(ring.index(z) + step) % n] for z in range(n))


def run_copies(copies, product, cuts, total):
    for c, (low, high) in enumerate(zip(cuts, cuts[1:])):
        for copy in copies[c]:
            copy.wait()
        term = product(low, high)
        total[...] = total[...] + term if c else term


def project_kernel(n, tables, cuts, test_ref, inverse_ref, *rest):
    outs, (test_buf, buf, total, test_sems, sems) = rest[:-5], rest[-5:]
    me = lax.axis_index("dp")
    width = outs[0].shape[1]
    half = n // 2
    near = me // half * half
    if tables:
        runs = [((half - near) * width, half * width)]
        runs += [((near + (me + j) % half) * width, width) for j in range(1, half)]
    else:
        runs = [(me * width, width)]
    copies = []
    for c, (low, high) in enumerate(zip(cuts, cuts[1:])):
        part = pl.ds(low, high - low)
        copies.append([pltpu.make_async_copy(test_ref.at[0, :, part], test_buf.at[:, part], test_sems.at[c])])
        copies[c][0].start()
        at = 0
        for i, (first, span) in enumerate(runs):
            source = inverse_ref.at[0, part, pl.ds(pl.multiple_of(first, span), span)]
            copies[c].append(pltpu.make_async_copy(source, buf.at[part, pl.ds(at, span)], sems.at[c, i]))
            copies[c][-1].start(priority=1)
            at += span

    def product(low, high):
        return jnp.dot(test_buf[:, low:high], buf[low:high, :], preferred_element_type=jnp.float32)

    run_copies(copies, product, cuts, total)
    if not tables:
        outs[0][...] = total[...]
        return
    for table, out in zip(tables, outs):
        block = pick(table, me)
        place = jnp.where(block // half == me // half, half + (block - me + half) % half - 1, block % half)
        out[...] = total[:, pl.ds(pl.multiple_of(place * width, width), width)].astype(out.dtype)


def project(n, tables, out_dtype, test, inverse):
    tests, depth = test.shape[1:]
    width = inverse.shape[2] // n
    count = max(len(tables), 1)
    runs = n // 2 if tables else 1
    rows = min(depth, 2 * LANES)
    cuts = list(range(0, depth, rows)) + [depth]
    if cuts[-1] - cuts[-2] == 2 * LANES:
        cuts.insert(-1, depth - LANES)
    return pl.pallas_call(
        functools.partial(project_kernel, n, tables, cuts),
        in_specs=[ANY, ANY],
        out_specs=[VMEM] * count,
        out_shape=[jax.ShapeDtypeStruct((tests, width), out_dtype)] * count,
        scratch_shapes=[
            pltpu.VMEM((tests, depth), test.dtype),
            pltpu.VMEM((depth, width * count), inverse.dtype),
            pltpu.VMEM((tests, width * count), jnp.float32),
            pltpu.SemaphoreType.DMA((len(cuts) - 1,)),
            pltpu.SemaphoreType.DMA((len(cuts) - 1, runs)),
        ],
        compiler_params=pltpu.CompilerParams(vmem_limit_bytes=215 * MIB // 4),
        cost_estimate=pl.CostEstimate(
            flops=2 * tests * depth * width * count, bytes_accessed=2 * depth * width * count, transcendentals=0
        ),
        name="project",
    )(test, inverse)


def score_kernel(tables, parts, axes, *refs):
    count = len(tables)
    blocks, train_ref, refs = refs[:count], refs[count], refs[count + 1 :]
    me = lax.axis_index("dp")
    width = blocks[0].shape[1]
    contract = (((1,), (1,)), ((), ()))
    value = None
    for table, block in zip(tables, blocks):
        columns = pl.ds(pl.multiple_of(pick(table, me) * width, width), width)
        term = lax.dot_general(block[...], train_ref[0, :, columns], contract, preferred_element_type=jnp.float32)
        value = term if value is None else value + term
    if not parts:
        refs[0][...] = value
        return
    so_far, weight_ref, outs, raw = refs[0], refs[1], refs[2:-1], refs[-1]
    raw[...] = (so_far[...] + value) * weight_ref[...]
    place = lax.axis_index(axes[0]) * lax.axis_size(axes[1]) + lax.axis_index(axes[1])
    rows = outs[0].shape[0]
    for step, out in enumerate(outs):
        out[...] = raw[pl.ds(pl.multiple_of(lax.bitwise_xor(place, step) * rows, rows), rows), :]


def score(tables, parts, axes, blocks, train, *more):
    tests, width = blocks[0].shape
    columns = train.shape[1]
    count = len(blocks)
    outs = max(parts, 1)
    return pl.pallas_call(
        functools.partial(score_kernel, tables, parts, axes),
        in_specs=[VMEM] * (count + 1 + len(more)),
        out_specs=[VMEM] * outs,
        out_shape=[jax.ShapeDtypeStruct((tests // outs, columns), jnp.float32)] * outs,
        scratch_shapes=[pltpu.VMEM((tests, columns), jnp.float32)] * bool(parts),
        compiler_params=pltpu.CompilerParams(vmem_limit_bytes=16 * MIB),
        cost_estimate=pl.CostEstimate(
            flops=2 * count * tests * columns * width, bytes_accessed=2 * count * columns * width, transcendentals=0
        ),
        name="score",
    )(*blocks, train, *more)


def send(x, axes, table):
    return lax.ppermute(x, axes, list(enumerate(table)))


def line_shards(n, parts, axes, test_feat, kernel_inverse, train_feat, residual_weight):
    out_tables = [folded_ring(n, step) for step in range(1, n)]
    away = project(n, out_tables, jnp.bfloat16, test_feat, kernel_inverse)
    terms = [send(block, "dp", table) for table, block in zip(out_tables, away)]
    (total,) = project(n, [], jnp.float32, test_feat, kernel_inverse)
    for term in terms:
        total = total + term
    total = total.astype(jnp.bfloat16)
    back_tables = [plain_ring(n, step) for step in range(1, n)]
    blocks = [total] + [send(total, "dp", table) for table in back_tables]
    owners = [plain_ring(n, 0)] + [sources(table) for table in back_tables]
    (raw,) = score(owners[:2], 0, axes, blocks[:2], train_feat)
    rows = score(owners[2:], parts, axes, blocks[2:], train_feat, raw, residual_weight)
    result = rows[0]
    for step in (parts - 1, *range(1, parts - 1)):
        result = result + send(rows[step], axes, [z ^ step for z in range(parts)])
    return result


def general_shards(test_feat, kernel_inverse, train_feat, residual_weight):
    partial_sum = jnp.dot(test_feat[0], kernel_inverse[0], preferred_element_type=jnp.float32)
    projected = lax.psum(partial_sum, "dp").astype(jnp.bfloat16)
    raw = jnp.einsum("tf,nf->tn", projected, train_feat[0], preferred_element_type=jnp.float32)
    totals = raw * residual_weight[0][None, :]
    return lax.psum_scatter(totals, ("feat", "ens"), scatter_dimension=0, tiled=True)


def solution(mesh):
    in_specs = (
        P("ens", "groups", "dp"),
        P("ens", "dp", "feat"),
        P("ens", "dp", "feat"),
        P("ens", "dp"),
    )
    out_specs = P(("groups", "feat", "ens"), "dp")
    line, axes = mesh.shape["dp"], ("feat", "ens")
    parts = mesh.shape["feat"] * mesh.shape["ens"]
    if 2 < line <= SHORT_LINE and line % 2 == 0 and parts > 2 and parts & (parts - 1) == 0:
        body = functools.partial(line_shards, line, parts, axes)
    else:
        body = general_shards
    return jax.shard_map(body, mesh=mesh, in_specs=in_specs, out_specs=out_specs, check_vma=False)
```

time: 29.3 us -> 28.5 us (0.973)
  waiting for transfers between devices: 7.46 us -> 4.1 us
  starting transfers between devices: 12.1 us -> 14.9 us
    ppermute x9, waiting for transfers between devices: 7.46 us -> 4.1 us  [send(): return lax.ppermute(x, axes, list(enumerate(table)))]
    ppermute x9, starting transfers between devices: 12.1 us -> 14.9 us  [send(): return lax.ppermute(x, axes, list(enumerate(table)))]
  transfers between devices with their start and end apart: 9 -> 9, of which waited for: 6 -> 7; matrix products, arithmetic and copies ran while one was open for 0% -> 0% of each run, Pallas kernels for 10% -> 10%
where the time goes in v4:
time: 28.5 us; the launch traced here: 28.4 us
  starting transfers between devices  14.9 us (52%)
  Pallas kernels  8.66 us (30%)
  waiting for transfers between devices  4.1 us (14%)
  other arithmetic  0.64 us (2%)
    ppermute x9, starting transfers between devices, send(): return lax.ppermute(x, axes, list(enumerate(table)))  14.9 us
    pallas_call x2, Pallas kernels, project(): pl.pallas_call(functools.partial(project_kernel, n, tables, cuts), in_spe...  7.83 us
    ppermute x9, waiting for transfers between devices, send(): return lax.ppermute(x, axes, list(enumerate(table)))  4.1 us
    pallas_call x2, Pallas kernels, score(): pl.pallas_call(functools.partial(score_kernel, tables, parts, axes), in_s...  0.83 us
    add x1, other arithmetic, line_shards(): result = result + send(rows[step], axes, [z ^ step for z in range(parts)])  0.6 us
  transfers between devices with their start and end apart: 9, of which 7 were waited for; matrix products, arithmetic and copies ran while one was open for 0% of the time, Pallas kernels for 10%

profile of v4, /device:TPU:0, one launch (start us, length us, event | category | flops | bytes accessed | tf_op | source)
XLA Modules:
  0.0 28.4 jit_solution(14316018776897932659)
XLA Ops:
  0.0 5.3 %project.3 = (bf16[32,1024]{1,0:T(8,128)(2,1)S(1)}, bf16[32,1024]{1,0:T(8,128)(2,1)S(1)}, bf16[32,1024]{1,0:T(8,128)(2,1)S(1)}) custom-call(bf16[1,32,2048]{2,1,0:T(8,128)(2,1)} %test_ref.3, bf16[1,2048,4096]{2,1,0:T(8,128)(2,1)} %inverse_ref.3), custom_call_target="tpu_custom_call" | custom-call | flops 402653184 | bytes 12582912 | tf_op jit(solution)/shard_map/project/pallas_call | solution.py:90
  5.3 3.1 %collective-permute-start = (bf16[32,1024]{1,0:T(8,128)(2,1)S(1)}, bf16[32,1024]{1,0:T(8,128)(2,1)S(1)}, u32[]{:S(2)}, u32[]{:S(2)}) collective-permute-start(bf16[32,1024]{1,0:T(8,128)(2,1)S(1)} %get-tuple-element.12), channel_id=1, source_target_pairs={{0,4},{4,12},{8,0},{12,8},{1,5},{5,13},{9,1},{13,9},{2,6},{6,14},{... | collective-permute-start | bytes 196616 | tf_op jit(solution)/shard_map/ppermute | solution.py:152
  8.4 2.5 %collective-permute-start.1 = (bf16[32,1024]{1,0:T(8,128)(2,1)S(1)}, bf16[32,1024]{1,0:T(8,128)(2,1)S(1)}, u32[]{:S(2)}, u32[]{:S(2)}) collective-permute-start(bf16[32,1024]{1,0:T(8,128)(2,1)S(1)} %get-tuple-element.13), channel_id=1, source_target_pairs={{0,12},{4,8},{8,4},{12,0},{1,13},{5,9},{9,5},{13,1},{2,14},{6,10},... | collective-permute-start | bytes 196616 | tf_op jit(solution)/shard_map/ppermute | solution.py:152
  10.8 1.6 %collective-permute-start.2 = (bf16[32,1024]{1,0:T(8,128)(2,1)S(1)}, bf16[32,1024]{1,0:T(8,128)(2,1)S(1)}, u32[]{:S(2)}, u32[]{:S(2)}) collective-permute-start(bf16[32,1024]{1,0:T(8,128)(2,1)S(1)} %get-tuple-element.14), channel_id=1, source_target_pairs={{0,8},{4,0},{8,12},{12,4},{1,9},{5,1},{9,13},{13,5},{2,10},{6,2},{... | collective-permute-start | bytes 196616 | tf_op jit(solution)/shard_map/ppermute | solution.py:152
  12.4 2.6 %project.2 = f32[32,1024]{1,0:T(8,128)S(1)} custom-call(bf16[1,32,2048]{2,1,0:T(8,128)(2,1)} %test_ref.3, bf16[1,2048,4096]{2,1,0:T(8,128)(2,1)} %inverse_ref.3), custom_call_target="tpu_custom_call" | custom-call | flops 134217728 | bytes 4194304 | tf_op jit(solution)/shard_map/project/pallas_call | solution.py:90
  15.0 0.0 collective-permute-done
  15.0 0.3 %collective-permute-done.1 = bf16[32,1024]{1,0:T(8,128)(2,1)S(1)} collective-permute-done((bf16[32,1024]{1,0:T(8,128)(2,1)S(1)}, bf16[32,1024]{1,0:T(8,128)(2,1)S(1)}, u32[]{:S(2)}, u32[]{:S(2)}) %collective-permute-start.1) | collective-permute-done | bytes 65568 | tf_op jit(solution)/shard_map/ppermute | solution.py:152
  15.3 0.2 collective-permute-done.2
  15.6 1.7 %collective-permute-start.5 = (bf16[32,1024]{1,0:T(8,128)(2,1)S(1)}, bf16[32,1024]{1,0:T(8,128)(2,1)S(1)}, u32[]{:S(2)}, u32[]{:S(2)}) collective-permute-start(bf16[32,1024]{1,0:T(8,128)(2,1)S(1)} %add_convert_fusion.refs_0_), channel_id=1, source_target_pairs={{0,4},{4,8},{8,12},{12,0},{1,5},{5,9},{9,13},{13,1},{2,6},{6,10},{... | collective-permute-start | bytes 196616 | tf_op jit(solution)/shard_map/ppermute | solution.py:152
  17.3 2.0 %collective-permute-start.3 = (bf16[32,1024]{1,0:T(8,128)(2,1)S(1)}, bf16[32,1024]{1,0:T(8,128)(2,1)S(1)}, u32[]{:S(2)}, u32[]{:S(2)}) collective-permute-start(bf16[32,1024]{1,0:T(8,128)(2,1)S(1)} %add_convert_fusion.refs_0_), channel_id=1, source_target_pairs={{0,8},{4,12},{8,0},{12,4},{1,9},{5,13},{9,1},{13,5},{2,10},{6,14},... | collective-permute-start | bytes 196616 | tf_op jit(solution)/shard_map/ppermute | solution.py:152
  19.3 2.2 %collective-permute-start.4 = (bf16[32,1024]{1,0:T(8,128)(2,1)S(1)}, bf16[32,1024]{1,0:T(8,128)(2,1)S(1)}, u32[]{:S(2)}, u32[]{:S(2)}) collective-permute-start(bf16[32,1024]{1,0:T(8,128)(2,1)S(1)} %add_convert_fusion.refs_0_), channel_id=1, source_target_pairs={{0,12},{4,0},{8,4},{12,8},{1,13},{5,1},{9,5},{13,9},{2,14},{6,2},{... | collective-permute-start | bytes 196616 | tf_op jit(solution)/shard_map/ppermute | solution.py:152
  21.4 0.4 %collective-permute-done.5.refs_1_ = bf16[32,1024]{1,0:T(8,128)(2,1)S(1)} collective-permute-done((bf16[32,1024]{1,0:T(8,128)(2,1)S(1)}, bf16[32,1024]{1,0:T(8,128)(2,1)S(1)}, u32[]{:S(2)}, u32[]{:S(2)}) %collective-permute-start.5) | collective-permute-done | bytes 65568 | tf_op jit(solution)/shard_map/ppermute | solution.py:152
  21.9 0.0 copy-done
  21.9 0.4 %score.2.refs_3_ = f32[32,256]{1,0:T(8,128)S(1)} custom-call(bf16[32,1024]{1,0:T(8,128)(2,1)S(1)} %add_convert_fusion.refs_0_, bf16[32,1024]{1,0:T(8,128)(2,1)S(1)} %collective-permute-done.5.refs_1_, bf16[1,256,4096]{2,1,0:T(8,128)(2,1)S(1)} %copy-done), custom_call_target="tpu_custom_call" | custom-call | flops 33554432 | bytes 1048576 | tf_op jit(solution)/shard_map/score/pallas_call | solution.py:137
  22.3 0.4 %collective-permute-done.3.refs_0_ = bf16[32,1024]{1,0:T(8,128)(2,1)S(1)} collective-permute-done((bf16[32,1024]{1,0:T(8,128)(2,1)S(1)}, bf16[32,1024]{1,0:T(8,128)(2,1)S(1)}, u32[]{:S(2)}, u32[]{:S(2)}) %collective-permute-start.3) | collective-permute-done | bytes 65568 | tf_op jit(solution)/shard_map/ppermute | solution.py:152
  22.7 0.8 %collective-permute-done.4.refs_1_ = bf16[32,1024]{1,0:T(8,128)(2,1)S(1)} collective-permute-done((bf16[32,1024]{1,0:T(8,128)(2,1)S(1)}, bf16[32,1024]{1,0:T(8,128)(2,1)S(1)}, u32[]{:S(2)}, u32[]{:S(2)}) %collective-permute-start.4) | collective-permute-done | bytes 65568 | tf_op jit(solution)/shard_map/ppermute | solution.py:152
  23.6 0.4 %score.3 = (f32[8,256]{1,0:T(8,128)S(1)}, f32[8,256]{1,0:T(8,128)S(1)}, f32[8,256]{1,0:T(8,128)S(1)}, f32[8,256]{1,0:T(8,128)S(1)}) custom-call(bf16[32,1024]{1,0:T(8,128)(2,1)S(1)} %collective-permute-done.3.refs_0_, bf16[32,1024]{1,0:T(8,128)(2,1)S(1)} %collective-permute-done.4.refs_1_, bf16[1,256,4096]{2,1,0:T(8,128)(2,1)S(1)} %copy-done, ...), custom_call_target="tpu_custom_call" | custom-call | flops 33554432 | bytes 1048576 | tf_op jit(solution)/shard_map/score/pallas_call | solution.py:137
  24.0 0.1 collective-permute-start.6
  24.1 1.6 %collective-permute-start.7 = (f32[8,256]{1,0:T(8,128)S(1)}, f32[8,256]{1,0:T(8,128)S(1)}, u32[]{:S(2)}, u32[]{:S(2)}) collective-permute-start(f32[8,256]{1,0:T(8,128)S(1)} %get-tuple-element.17), channel_id=1, source_target_pairs={{0,1},{1,0},{2,3},{3,2},{4,5},{5,4},{6,7},{7,6},{8,9},{9,8},{10,11... | collective-permute-start | bytes 24584 | tf_op jit(solution)/shard_map/ppermute | solution.py:152
  25.6 0.3 %collective-permute-start.8 = (f32[8,256]{1,0:T(8,128)S(1)}, f32[8,256]{1,0:T(8,128)S(1)}, u32[]{:S(2)}, u32[]{:S(2)}) collective-permute-start(f32[8,256]{1,0:T(8,128)S(1)} %get-tuple-element.18), channel_id=1, source_target_pairs={{0,2},{1,3},{2,0},{3,1},{4,6},{5,7},{6,4},{7,5},{8,10},{9,11},{10,... | collective-permute-start | bytes 24584 | tf_op jit(solution)/shard_map/ppermute | solution.py:152
  25.9 1.3 %collective-permute-done.6 = f32[8,256]{1,0:T(8,128)S(1)} collective-permute-done((f32[8,256]{1,0:T(8,128)S(1)}, f32[8,256]{1,0:T(8,128)S(1)}, u32[]{:S(2)}, u32[]{:S(2)}) %collective-permute-start.6) | collective-permute-done | bytes 8224 | tf_op jit(solution)/shard_map/ppermute | solution.py:152
  27.2 0.6 %collective-permute-done.7 = f32[8,256]{1,0:T(8,128)S(1)} collective-permute-done((f32[8,256]{1,0:T(8,128)S(1)}, f32[8,256]{1,0:T(8,128)S(1)}, u32[]{:S(2)}, u32[]{:S(2)}) %collective-permute-start.7) | collective-permute-done | bytes 8224 | tf_op jit(solution)/shard_map/ppermute | solution.py:152
  27.8 0.0 collective-permute-done.8
  27.8 0.6 %add_add_fusion = f32[8,256]{1,0:T(8,128)} fusion(f32[8,256]{1,0:T(8,128)S(1)} %collective-permute-done.8, f32[8,256]{1,0:T(8,128)S(1)} %collective-permute-done.7, f32[8,256]{1,0:T(8,128)S(1)} %get-tuple-element.15, f32[8,256]{1,0:T(8,128)S(1)} %collective-permute-done.6), kind=kLoop, calls=%fused_computation.1 | loop fusion | flops 6144 | bytes 40960 | tf_op jit(solution)/shard_map/add | solution.py:170
  (4 shorter events, 0.0 us)
Async XLA Ops:
  0.0 21.9 %copy-start = (bf16[1,256,4096]{2,1,0:T(8,128)(2,1)S(1)}, bf16[1,256,4096]{2,1,0:T(8,128)(2,1)}, u32[]{:S(2)}) copy-start(bf16[1,256,4096]{2,1,0:T(8,128)(2,1)} %refs_2_.3) | copy-start | bytes 6291460
  0.0 23.6 %copy-start.1 = (f32[1,256]{1,0:T(1,128)S(1)}, f32[1,256]{1,0:T(1,128)}, u32[]{:S(2)}) copy-start(f32[1,256]{1,0:T(1,128)} %refs_4_.1) | copy-start | bytes 3076
  5.3 9.7 %collective-permute-start = (bf16[32,1024]{1,0:T(8,128)(2,1)S(1)}, bf16[32,1024]{1,0:T(8,128)(2,1)S(1)}, u32[]{:S(2)}, u32[]{:S(2)}) collective-permute-start(bf16[32,1024]{1,0:T(8,128)(2,1)S(1)} %get-tuple-element.12), channel_id=1, source_target_pairs={{0,4},{4,12},{8,0},{12,8},{1,5},{5,13},{9,1},{13,9},{2,6},{6,14},{... | collective-permute-start | bytes 196616 | tf_op jit(solution)/shard_map/ppermute | solution.py:152
  8.4 7.0 %collective-permute-start.1 = (bf16[32,1024]{1,0:T(8,128)(2,1)S(1)}, bf16[32,1024]{1,0:T(8,128)(2,1)S(1)}, u32[]{:S(2)}, u32[]{:S(2)}) collective-permute-start(bf16[32,1024]{1,0:T(8,128)(2,1)S(1)} %get-tuple-element.13), channel_id=1, source_target_pairs={{0,12},{4,8},{8,4},{12,0},{1,13},{5,9},{9,5},{13,1},{2,14},{6,10},... | collective-permute-start | bytes 196616 | tf_op jit(solution)/shard_map/ppermute | solution.py:152
  10.8 4.7 %collective-permute-start.2 = (bf16[32,1024]{1,0:T(8,128)(2,1)S(1)}, bf16[32,1024]{1,0:T(8,128)(2,1)S(1)}, u32[]{:S(2)}, u32[]{:S(2)}) collective-permute-start(bf16[32,1024]{1,0:T(8,128)(2,1)S(1)} %get-tuple-element.14), channel_id=1, source_target_pairs={{0,8},{4,0},{8,12},{12,4},{1,9},{5,1},{9,13},{13,5},{2,10},{6,2},{... | collective-permute-start | bytes 196616 | tf_op jit(solution)/shard_map/ppermute | solution.py:152
  15.6 6.3 %collective-permute-start.5 = (bf16[32,1024]{1,0:T(8,128)(2,1)S(1)}, bf16[32,1024]{1,0:T(8,128)(2,1)S(1)}, u32[]{:S(2)}, u32[]{:S(2)}) collective-permute-start(bf16[32,1024]{1,0:T(8,128)(2,1)S(1)} %add_convert_fusion.refs_0_), channel_id=1, source_target_pairs={{0,4},{4,8},{8,12},{12,0},{1,5},{5,9},{9,13},{13,1},{2,6},{6,10},{... | collective-permute-start | bytes 196616 | tf_op jit(solution)/shard_map/ppermute | solution.py:152
  17.3 5.5 %collective-permute-start.3 = (bf16[32,1024]{1,0:T(8,128)(2,1)S(1)}, bf16[32,1024]{1,0:T(8,128)(2,1)S(1)}, u32[]{:S(2)}, u32[]{:S(2)}) collective-permute-start(bf16[32,1024]{1,0:T(8,128)(2,1)S(1)} %add_convert_fusion.refs_0_), channel_id=1, source_target_pairs={{0,8},{4,12},{8,0},{12,4},{1,9},{5,13},{9,1},{13,5},{2,10},{6,14},... | collective-permute-start | bytes 196616 | tf_op jit(solution)/shard_map/ppermute | solution.py:152
  19.3 4.3 %collective-permute-start.4 = (bf16[32,1024]{1,0:T(8,128)(2,1)S(1)}, bf16[32,1024]{1,0:T(8,128)(2,1)S(1)}, u32[]{:S(2)}, u32[]{:S(2)}) collective-permute-start(bf16[32,1024]{1,0:T(8,128)(2,1)S(1)} %add_convert_fusion.refs_0_), channel_id=1, source_target_pairs={{0,12},{4,0},{8,4},{12,8},{1,13},{5,1},{9,5},{13,9},{2,14},{6,2},{... | collective-permute-start | bytes 196616 | tf_op jit(solution)/shard_map/ppermute | solution.py:152
  24.0 3.2 %collective-permute-start.6 = (f32[8,256]{1,0:T(8,128)S(1)}, f32[8,256]{1,0:T(8,128)S(1)}, u32[]{:S(2)}, u32[]{:S(2)}) collective-permute-start(f32[8,256]{1,0:T(8,128)S(1)} %get-tuple-element.16), channel_id=1, source_target_pairs={{0,3},{1,2},{2,1},{3,0},{4,7},{5,6},{6,5},{7,4},{8,11},{9,10},{10,... | collective-permute-start | bytes 24584 | tf_op jit(solution)/shard_map/ppermute | solution.py:152
  24.1 3.7 %collective-permute-start.7 = (f32[8,256]{1,0:T(8,128)S(1)}, f32[8,256]{1,0:T(8,128)S(1)}, u32[]{:S(2)}, u32[]{:S(2)}) collective-permute-start(f32[8,256]{1,0:T(8,128)S(1)} %get-tuple-element.17), channel_id=1, source_target_pairs={{0,1},{1,0},{2,3},{3,2},{4,5},{5,4},{6,7},{7,6},{8,9},{9,8},{10,11... | collective-permute-start | bytes 24584 | tf_op jit(solution)/shard_map/ppermute | solution.py:152
  25.6 2.2 %collective-permute-start.8 = (f32[8,256]{1,0:T(8,128)S(1)}, f32[8,256]{1,0:T(8,128)S(1)}, u32[]{:S(2)}, u32[]{:S(2)}) collective-permute-start(f32[8,256]{1,0:T(8,128)S(1)} %get-tuple-element.18), channel_id=1, source_target_pairs={{0,2},{1,3},{2,0},{3,1},{4,6},{5,7},{6,4},{7,5},{8,10},{9,11},{10,... | collective-permute-start | bytes 24584 | tf_op jit(solution)/shard_map/ppermute | solution.py:152

commit v5 on v4

--- a/solution.py
+++ b/solution.py
@@ -119,7 +119,7 @@
         term = lax.dot_general(block[...], train_ref[0, :, columns], contract, preferred_element_type=jnp.float32)
         value = term if value is None else value + term
     if not parts:
-        refs[0][...] = value
+        refs[-1][...] = value if len(refs) == 1 else refs[0][...] + value
         return
     so_far, weight_ref, outs, raw = refs[0], refs[1], refs[2:-1], refs[-1]
     raw[...] = (so_far[...] + value) * weight_ref[...]
@@ -164,7 +164,9 @@
     blocks = [total] + [send(total, "dp", table) for table in back_tables]
     owners = [plain_ring(n, 0)] + [sources(table) for table in back_tables]
     (raw,) = score(owners[:2], 0, axes, blocks[:2], train_feat)
-    rows = score(owners[2:], parts, axes, blocks[2:], train_feat, raw, residual_weight)
+    for i in range(2, n - 1):
+        (raw,) = score(owners[i : i + 1], 0, axes, blocks[i : i + 1], train_feat, raw)
+    rows = score(owners[n - 1 :], parts, axes, blocks[n - 1 :], train_feat, raw, residual_weight)
     result = rows[0]
     for step in (parts - 1, *range(1, parts - 1)):
         result = result + send(rows[step], axes, [z ^ step for z in range(parts)])

time: 28.5 us -> 28.4 us (level)
    pallas_call x2 -> x3, Pallas kernels: 0.83 us -> 0.91 us  [score(): pl.pallas_call(functools.partial(score_kernel, tables, parts, axes), in_s...]
  transfers between devices with their start and end apart: 9 -> 9, of which waited for: 7 -> 7; matrix products, arithmetic and copies ran while one was open for 0% -> 0% of each run, Pallas kernels for 10% -> 11%
where the time goes in v5:
time: 28.4 us; the launch traced here: 28.2 us
  starting transfers between devices  14.9 us (52%)
  Pallas kernels  8.74 us (31%)
  waiting for transfers between devices  3.86 us (14%)
  other arithmetic  0.64 us (2%)
    ppermute x9, starting transfers between devices, send(): return lax.ppermute(x, axes, list(enumerate(table)))  14.9 us
    pallas_call x2, Pallas kernels, project(): pl.pallas_call(functools.partial(project_kernel, n, tables, cuts), in_spe...  7.83 us
    ppermute x9, waiting for transfers between devices, send(): return lax.ppermute(x, axes, list(enumerate(table)))  3.86 us
    pallas_call x3, Pallas kernels, score(): pl.pallas_call(functools.partial(score_kernel, tables, parts, axes), in_s...  0.91 us
    add x1, other arithmetic, line_shards(): result = result + send(rows[step], axes, [z ^ step for z in range(parts)])  0.6 us
  transfers between devices with their start and end apart: 9, of which 7 were waited for; matrix products, arithmetic and copies ran while one was open for 0% of the time, Pallas kernels for 11%

profile of v5, /device:TPU:0, one launch (start us, length us, event | category | flops | bytes accessed | tf_op | source)
XLA Modules:
  0.0 28.2 jit_solution(17287632040396124294)
XLA Ops:
  0.0 5.3 %project.3 = (bf16[32,1024]{1,0:T(8,128)(2,1)S(1)}, bf16[32,1024]{1,0:T(8,128)(2,1)S(1)}, bf16[32,1024]{1,0:T(8,128)(2,1)S(1)}) custom-call(bf16[1,32,2048]{2,1,0:T(8,128)(2,1)} %test_ref.3, bf16[1,2048,4096]{2,1,0:T(8,128)(2,1)} %inverse_ref.3), custom_call_target="tpu_custom_call" | custom-call | flops 402653184 | bytes 12582912 | tf_op jit(solution)/shard_map/project/pallas_call | solution.py:90
  5.3 3.1 %collective-permute-start = (bf16[32,1024]{1,0:T(8,128)(2,1)S(1)}, bf16[32,1024]{1,0:T(8,128)(2,1)S(1)}, u32[]{:S(2)}, u32[]{:S(2)}) collective-permute-start(bf16[32,1024]{1,0:T(8,128)(2,1)S(1)} %get-tuple-element.12), channel_id=1, source_target_pairs={{0,4},{4,12},{8,0},{12,8},{1,5},{5,13},{9,1},{13,9},{2,6},{6,14},{... | collective-permute-start | bytes 196616 | tf_op jit(solution)/shard_map/ppermute | solution.py:152
  8.4 2.5 %collective-permute-start.1 = (bf16[32,1024]{1,0:T(8,128)(2,1)S(1)}, bf16[32,1024]{1,0:T(8,128)(2,1)S(1)}, u32[]{:S(2)}, u32[]{:S(2)}) collective-permute-start(bf16[32,1024]{1,0:T(8,128)(2,1)S(1)} %get-tuple-element.13), channel_id=1, source_target_pairs={{0,12},{4,8},{8,4},{12,0},{1,13},{5,9},{9,5},{13,1},{2,14},{6,10},... | collective-permute-start | bytes 196616 | tf_op jit(solution)/shard_map/ppermute | solution.py:152
  10.8 1.6 %collective-permute-start.2 = (bf16[32,1024]{1,0:T(8,128)(2,1)S(1)}, bf16[32,1024]{1,0:T(8,128)(2,1)S(1)}, u32[]{:S(2)}, u32[]{:S(2)}) collective-permute-start(bf16[32,1024]{1,0:T(8,128)(2,1)S(1)} %get-tuple-element.14), channel_id=1, source_target_pairs={{0,8},{4,0},{8,12},{12,4},{1,9},{5,1},{9,13},{13,5},{2,10},{6,2},{... | collective-permute-start | bytes 196616 | tf_op jit(solution)/shard_map/ppermute | solution.py:152
  12.4 2.6 %project.2 = f32[32,1024]{1,0:T(8,128)S(1)} custom-call(bf16[1,32,2048]{2,1,0:T(8,128)(2,1)} %test_ref.3, bf16[1,2048,4096]{2,1,0:T(8,128)(2,1)} %inverse_ref.3), custom_call_target="tpu_custom_call" | custom-call | flops 134217728 | bytes 4194304 | tf_op jit(solution)/shard_map/project/pallas_call | solution.py:90
  15.0 0.0 collective-permute-done
  15.0 0.3 %collective-permute-done.1 = bf16[32,1024]{1,0:T(8,128)(2,1)S(1)} collective-permute-done((bf16[32,1024]{1,0:T(8,128)(2,1)S(1)}, bf16[32,1024]{1,0:T(8,128)(2,1)S(1)}, u32[]{:S(2)}, u32[]{:S(2)}) %collective-permute-start.1) | collective-permute-done | bytes 65568 | tf_op jit(solution)/shard_map/ppermute | solution.py:152
  15.3 0.2 collective-permute-done.2
  15.6 1.7 %collective-permute-start.5 = (bf16[32,1024]{1,0:T(8,128)(2,1)S(1)}, bf16[32,1024]{1,0:T(8,128)(2,1)S(1)}, u32[]{:S(2)}, u32[]{:S(2)}) collective-permute-start(bf16[32,1024]{1,0:T(8,128)(2,1)S(1)} %add_convert_fusion.refs_0_), channel_id=1, source_target_pairs={{0,4},{4,8},{8,12},{12,0},{1,5},{5,9},{9,13},{13,1},{2,6},{6,10},{... | collective-permute-start | bytes 196616 | tf_op jit(solution)/shard_map/ppermute | solution.py:152
  17.3 2.0 %collective-permute-start.4 = (bf16[32,1024]{1,0:T(8,128)(2,1)S(1)}, bf16[32,1024]{1,0:T(8,128)(2,1)S(1)}, u32[]{:S(2)}, u32[]{:S(2)}) collective-permute-start(bf16[32,1024]{1,0:T(8,128)(2,1)S(1)} %add_convert_fusion.refs_0_), channel_id=1, source_target_pairs={{0,8},{4,12},{8,0},{12,4},{1,9},{5,13},{9,1},{13,5},{2,10},{6,14},... | collective-permute-start | bytes 196616 | tf_op jit(solution)/shard_map/ppermute | solution.py:152
  19.3 2.2 %collective-permute-start.3 = (bf16[32,1024]{1,0:T(8,128)(2,1)S(1)}, bf16[32,1024]{1,0:T(8,128)(2,1)S(1)}, u32[]{:S(2)}, u32[]{:S(2)}) collective-permute-start(bf16[32,1024]{1,0:T(8,128)(2,1)S(1)} %add_convert_fusion.refs_0_), channel_id=1, source_target_pairs={{0,12},{4,0},{8,4},{12,8},{1,13},{5,1},{9,5},{13,9},{2,14},{6,2},{... | collective-permute-start | bytes 196616 | tf_op jit(solution)/shard_map/ppermute | solution.py:152
  21.4 0.4 %collective-permute-done.5.refs_1_ = bf16[32,1024]{1,0:T(8,128)(2,1)S(1)} collective-permute-done((bf16[32,1024]{1,0:T(8,128)(2,1)S(1)}, bf16[32,1024]{1,0:T(8,128)(2,1)S(1)}, u32[]{:S(2)}, u32[]{:S(2)}) %collective-permute-start.5) | collective-permute-done | bytes 65568 | tf_op jit(solution)/shard_map/ppermute | solution.py:152
  21.9 0.4 %score.3.refs_2_ = f32[32,256]{1,0:T(8,128)S(1)} custom-call(bf16[32,1024]{1,0:T(8,128)(2,1)S(1)} %add_convert_fusion.refs_0_, bf16[32,1024]{1,0:T(8,128)(2,1)S(1)} %collective-permute-done.5.refs_1_, bf16[1,256,4096]{2,1,0:T(8,128)(2,1)S(1)} %copy-done), custom_call_target="tpu_custom_call" | custom-call | flops 33554432 | bytes 1048576 | tf_op jit(solution)/shard_map/score/pallas_call | solution.py:137
  22.3 0.4 %collective-permute-done.4.refs_0_ = bf16[32,1024]{1,0:T(8,128)(2,1)S(1)} collective-permute-done((bf16[32,1024]{1,0:T(8,128)(2,1)S(1)}, bf16[32,1024]{1,0:T(8,128)(2,1)S(1)}, u32[]{:S(2)}, u32[]{:S(2)}) %collective-permute-start.4) | collective-permute-done | bytes 65568 | tf_op jit(solution)/shard_map/ppermute | solution.py:152
  22.7 0.2 score.4.refs_2_
  22.9 0.6 %collective-permute-done.3.refs_0_ = bf16[32,1024]{1,0:T(8,128)(2,1)S(1)} collective-permute-done((bf16[32,1024]{1,0:T(8,128)(2,1)S(1)}, bf16[32,1024]{1,0:T(8,128)(2,1)S(1)}, u32[]{:S(2)}, u32[]{:S(2)}) %collective-permute-start.3) | collective-permute-done | bytes 65568 | tf_op jit(solution)/shard_map/ppermute | solution.py:152
  23.6 0.3 score.5
  23.8 0.1 collective-permute-start.6
  23.9 1.6 %collective-permute-start.7 = (f32[8,256]{1,0:T(8,128)S(1)}, f32[8,256]{1,0:T(8,128)S(1)}, u32[]{:S(2)}, u32[]{:S(2)}) collective-permute-start(f32[8,256]{1,0:T(8,128)S(1)} %get-tuple-element.17), channel_id=1, source_target_pairs={{0,1},{1,0},{2,3},{3,2},{4,5},{5,4},{6,7},{7,6},{8,9},{9,8},{10,11... | collective-permute-start | bytes 24584 | tf_op jit(solution)/shard_map/ppermute | solution.py:152
  25.5 0.3 %collective-permute-start.8 = (f32[8,256]{1,0:T(8,128)S(1)}, f32[8,256]{1,0:T(8,128)S(1)}, u32[]{:S(2)}, u32[]{:S(2)}) collective-permute-start(f32[8,256]{1,0:T(8,128)S(1)} %get-tuple-element.18), channel_id=1, source_target_pairs={{0,2},{1,3},{2,0},{3,1},{4,6},{5,7},{6,4},{7,5},{8,10},{9,11},{10,... | collective-permute-start | bytes 24584 | tf_op jit(solution)/shard_map/ppermute | solution.py:152
  25.8 1.3 %collective-permute-done.6 = f32[8,256]{1,0:T(8,128)S(1)} collective-permute-done((f32[8,256]{1,0:T(8,128)S(1)}, f32[8,256]{1,0:T(8,128)S(1)}, u32[]{:S(2)}, u32[]{:S(2)}) %collective-permute-start.6) | collective-permute-done | bytes 8224 | tf_op jit(solution)/shard_map/ppermute | solution.py:152
  27.0 0.6 %collective-permute-done.7 = f32[8,256]{1,0:T(8,128)S(1)} collective-permute-done((f32[8,256]{1,0:T(8,128)S(1)}, f32[8,256]{1,0:T(8,128)S(1)}, u32[]{:S(2)}, u32[]{:S(2)}) %collective-permute-start.7) | collective-permute-done | bytes 8224 | tf_op jit(solution)/shard_map/ppermute | solution.py:152
  27.6 0.0 collective-permute-done.8
  27.6 0.6 %add_add_fusion = f32[8,256]{1,0:T(8,128)} fusion(f32[8,256]{1,0:T(8,128)S(1)} %collective-permute-done.8, f32[8,256]{1,0:T(8,128)S(1)} %collective-permute-done.7, f32[8,256]{1,0:T(8,128)S(1)} %get-tuple-element.15, f32[8,256]{1,0:T(8,128)S(1)} %collective-permute-done.6), kind=kLoop, calls=%fused_computation.1 | loop fusion | flops 6144 | bytes 40960 | tf_op jit(solution)/shard_map/add | solution.py:172
  (5 shorter events, 0.0 us)
Async XLA Ops:
  0.0 21.9 %copy-start = (bf16[1,256,4096]{2,1,0:T(8,128)(2,1)S(1)}, bf16[1,256,4096]{2,1,0:T(8,128)(2,1)}, u32[]{:S(2)}) copy-start(bf16[1,256,4096]{2,1,0:T(8,128)(2,1)} %refs_1_.3) | copy-start | bytes 6291460
  0.0 23.6 %copy-start.1 = (f32[1,256]{1,0:T(1,128)S(1)}, f32[1,256]{1,0:T(1,128)}, u32[]{:S(2)}) copy-start(f32[1,256]{1,0:T(1,128)} %refs_3_.1) | copy-start | bytes 3076
  5.3 9.7 %collective-permute-start = (bf16[32,1024]{1,0:T(8,128)(2,1)S(1)}, bf16[32,1024]{1,0:T(8,128)(2,1)S(1)}, u32[]{:S(2)}, u32[]{:S(2)}) collective-permute-start(bf16[32,1024]{1,0:T(8,128)(2,1)S(1)} %get-tuple-element.12), channel_id=1, source_target_pairs={{0,4},{4,12},{8,0},{12,8},{1,5},{5,13},{9,1},{13,9},{2,6},{6,14},{... | collective-permute-start | bytes 196616 | tf_op jit(solution)/shard_map/ppermute | solution.py:152
  8.4 7.0 %collective-permute-start.1 = (bf16[32,1024]{1,0:T(8,128)(2,1)S(1)}, bf16[32,1024]{1,0:T(8,128)(2,1)S(1)}, u32[]{:S(2)}, u32[]{:S(2)}) collective-permute-start(bf16[32,1024]{1,0:T(8,128)(2,1)S(1)} %get-tuple-element.13), channel_id=1, source_target_pairs={{0,12},{4,8},{8,4},{12,0},{1,13},{5,9},{9,5},{13,1},{2,14},{6,10},... | collective-permute-start | bytes 196616 | tf_op jit(solution)/shard_map/ppermute | solution.py:152
  10.8 4.7 %collective-permute-start.2 = (bf16[32,1024]{1,0:T(8,128)(2,1)S(1)}, bf16[32,1024]{1,0:T(8,128)(2,1)S(1)}, u32[]{:S(2)}, u32[]{:S(2)}) collective-permute-start(bf16[32,1024]{1,0:T(8,128)(2,1)S(1)} %get-tuple-element.14), channel_id=1, source_target_pairs={{0,8},{4,0},{8,12},{12,4},{1,9},{5,1},{9,13},{13,5},{2,10},{6,2},{... | collective-permute-start | bytes 196616 | tf_op jit(solution)/shard_map/ppermute | solution.py:152
  15.6 6.3 %collective-permute-start.5 = (bf16[32,1024]{1,0:T(8,128)(2,1)S(1)}, bf16[32,1024]{1,0:T(8,128)(2,1)S(1)}, u32[]{:S(2)}, u32[]{:S(2)}) collective-permute-start(bf16[32,1024]{1,0:T(8,128)(2,1)S(1)} %add_convert_fusion.refs_0_), channel_id=1, source_target_pairs={{0,4},{4,8},{8,12},{12,0},{1,5},{5,9},{9,13},{13,1},{2,6},{6,10},{... | collective-permute-start | bytes 196616 | tf_op jit(solution)/shard_map/ppermute | solution.py:152
  17.3 5.5 %collective-permute-start.4 = (bf16[32,1024]{1,0:T(8,128)(2,1)S(1)}, bf16[32,1024]{1,0:T(8,128)(2,1)S(1)}, u32[]{:S(2)}, u32[]{:S(2)}) collective-permute-start(bf16[32,1024]{1,0:T(8,128)(2,1)S(1)} %add_convert_fusion.refs_0_), channel_id=1, source_target_pairs={{0,8},{4,12},{8,0},{12,4},{1,9},{5,13},{9,1},{13,5},{2,10},{6,14},... | collective-permute-start | bytes 196616 | tf_op jit(solution)/shard_map/ppermute | solution.py:152
  19.3 4.3 %collective-permute-start.3 = (bf16[32,1024]{1,0:T(8,128)(2,1)S(1)}, bf16[32,1024]{1,0:T(8,128)(2,1)S(1)}, u32[]{:S(2)}, u32[]{:S(2)}) collective-permute-start(bf16[32,1024]{1,0:T(8,128)(2,1)S(1)} %add_convert_fusion.refs_0_), channel_id=1, source_target_pairs={{0,12},{4,0},{8,4},{12,8},{1,13},{5,1},{9,5},{13,9},{2,14},{6,2},{... | collective-permute-start | bytes 196616 | tf_op jit(solution)/shard_map/ppermute | solution.py:152
  23.8 3.2 %collective-permute-start.6 = (f32[8,256]{1,0:T(8,128)S(1)}, f32[8,256]{1,0:T(8,128)S(1)}, u32[]{:S(2)}, u32[]{:S(2)}) collective-permute-start(f32[8,256]{1,0:T(8,128)S(1)} %get-tuple-element.16), channel_id=1, source_target_pairs={{0,3},{1,2},{2,1},{3,0},{4,7},{5,6},{6,5},{7,4},{8,11},{9,10},{10,... | collective-permute-start | bytes 24584 | tf_op jit(solution)/shard_map/ppermute | solution.py:152
  23.9 3.7 %collective-permute-start.7 = (f32[8,256]{1,0:T(8,128)S(1)}, f32[8,256]{1,0:T(8,128)S(1)}, u32[]{:S(2)}, u32[]{:S(2)}) collective-permute-start(f32[8,256]{1,0:T(8,128)S(1)} %get-tuple-element.17), channel_id=1, source_target_pairs={{0,1},{1,0},{2,3},{3,2},{4,5},{5,4},{6,7},{7,6},{8,9},{9,8},{10,11... | collective-permute-start | bytes 24584 | tf_op jit(solution)/shard_map/ppermute | solution.py:152
  25.5 2.2 %collective-permute-start.8 = (f32[8,256]{1,0:T(8,128)S(1)}, f32[8,256]{1,0:T(8,128)S(1)}, u32[]{:S(2)}, u32[]{:S(2)}) collective-permute-start(f32[8,256]{1,0:T(8,128)S(1)} %get-tuple-element.18), channel_id=1, source_target_pairs={{0,2},{1,3},{2,0},{3,1},{4,6},{5,7},{6,4},{7,5},{8,10},{9,11},{10,... | collective-permute-start | bytes 24584 | tf_op jit(solution)/shard_map/ppermute | solution.py:152

commit v6 on v5

--- a/solution.py
+++ b/solution.py
@@ -87,6 +87,7 @@
     cuts = list(range(0, depth, rows)) + [depth]
     if cuts[-1] - cuts[-2] == 2 * LANES:
         cuts.insert(-1, depth - LANES)
+        cuts.insert(1, LANES)
     return pl.pallas_call(
         functools.partial(project_kernel, n, tables, cuts),
         in_specs=[ANY, ANY],

time: 28.4 us -> 28.4 us (level)
  no operation moved by 1% of the time
where the time goes in v6:
time: 28.4 us; the launch traced here: 28.3 us
  starting transfers between devices  14.9 us (52%)
  Pallas kernels  8.79 us (31%)
  waiting for transfers between devices  3.84 us (14%)
  other arithmetic  0.64 us (2%)
    ppermute x9, starting transfers between devices, send(): return lax.ppermute(x, axes, list(enumerate(table)))  14.9 us
    pallas_call x2, Pallas kernels, project(): pl.pallas_call(functools.partial(project_kernel, n, tables, cuts), in_spe...  7.88 us
    ppermute x9, waiting for transfers between devices, send(): return lax.ppermute(x, axes, list(enumerate(table)))  3.84 us
    pallas_call x3, Pallas kernels, score(): pl.pallas_call(functools.partial(score_kernel, tables, parts, axes), in_s...  0.91 us
    add x1, other arithmetic, line_shards(): result = result + send(rows[step], axes, [z ^ step for z in range(parts)])  0.6 us
  transfers between devices with their start and end apart: 9, of which 7 were waited for; matrix products, arithmetic and copies ran while one was open for 0% of the time, Pallas kernels for 11%

profile of v6, /device:TPU:0, one launch (start us, length us, event | category | flops | bytes accessed | tf_op | source)
XLA Modules:
  0.0 28.3 jit_solution(6184163141253560849)
XLA Ops:
  0.0 5.3 %project.3 = (bf16[32,1024]{1,0:T(8,128)(2,1)S(1)}, bf16[32,1024]{1,0:T(8,128)(2,1)S(1)}, bf16[32,1024]{1,0:T(8,128)(2,1)S(1)}) custom-call(bf16[1,32,2048]{2,1,0:T(8,128)(2,1)} %test_ref.3, bf16[1,2048,4096]{2,1,0:T(8,128)(2,1)} %inverse_ref.3), custom_call_target="tpu_custom_call" | custom-call | flops 402653184 | bytes 12582912 | tf_op jit(solution)/shard_map/project/pallas_call | solution.py:91
  5.3 3.1 %collective-permute-start = (bf16[32,1024]{1,0:T(8,128)(2,1)S(1)}, bf16[32,1024]{1,0:T(8,128)(2,1)S(1)}, u32[]{:S(2)}, u32[]{:S(2)}) collective-permute-start(bf16[32,1024]{1,0:T(8,128)(2,1)S(1)} %get-tuple-element.12), channel_id=1, source_target_pairs={{0,4},{4,12},{8,0},{12,8},{1,5},{5,13},{9,1},{13,9},{2,6},{6,14},{... | collective-permute-start | bytes 196616 | tf_op jit(solution)/shard_map/ppermute | solution.py:153
  8.4 2.5 %collective-permute-start.1 = (bf16[32,1024]{1,0:T(8,128)(2,1)S(1)}, bf16[32,1024]{1,0:T(8,128)(2,1)S(1)}, u32[]{:S(2)}, u32[]{:S(2)}) collective-permute-start(bf16[32,1024]{1,0:T(8,128)(2,1)S(1)} %get-tuple-element.13), channel_id=1, source_target_pairs={{0,12},{4,8},{8,4},{12,0},{1,13},{5,9},{9,5},{13,1},{2,14},{6,10},... | collective-permute-start | bytes 196616 | tf_op jit(solution)/shard_map/ppermute | solution.py:153
  10.9 1.6 %collective-permute-start.2 = (bf16[32,1024]{1,0:T(8,128)(2,1)S(1)}, bf16[32,1024]{1,0:T(8,128)(2,1)S(1)}, u32[]{:S(2)}, u32[]{:S(2)}) collective-permute-start(bf16[32,1024]{1,0:T(8,128)(2,1)S(1)} %get-tuple-element.14), channel_id=1, source_target_pairs={{0,8},{4,0},{8,12},{12,4},{1,9},{5,1},{9,13},{13,5},{2,10},{6,2},{... | collective-permute-start | bytes 196616 | tf_op jit(solution)/shard_map/ppermute | solution.py:153
  12.4 2.6 %project.2 = f32[32,1024]{1,0:T(8,128)S(1)} custom-call(bf16[1,32,2048]{2,1,0:T(8,128)(2,1)} %test_ref.3, bf16[1,2048,4096]{2,1,0:T(8,128)(2,1)} %inverse_ref.3), custom_call_target="tpu_custom_call" | custom-call | flops 134217728 | bytes 4194304 | tf_op jit(solution)/shard_map/project/pallas_call | solution.py:91
  15.0 0.0 collective-permute-done
  15.0 0.3 %collective-permute-done.1 = bf16[32,1024]{1,0:T(8,128)(2,1)S(1)} collective-permute-done((bf16[32,1024]{1,0:T(8,128)(2,1)S(1)}, bf16[32,1024]{1,0:T(8,128)(2,1)S(1)}, u32[]{:S(2)}, u32[]{:S(2)}) %collective-permute-start.1) | collective-permute-done | bytes 65568 | tf_op jit(solution)/shard_map/ppermute | solution.py:153
  15.3 0.2 collective-permute-done.2
  15.6 1.7 %collective-permute-start.5 = (bf16[32,1024]{1,0:T(8,128)(2,1)S(1)}, bf16[32,1024]{1,0:T(8,128)(2,1)S(1)}, u32[]{:S(2)}, u32[]{:S(2)}) collective-permute-start(bf16[32,1024]{1,0:T(8,128)(2,1)S(1)} %add_convert_fusion.refs_0_), channel_id=1, source_target_pairs={{0,4},{4,8},{8,12},{12,0},{1,5},{5,9},{9,13},{13,1},{2,6},{6,10},{... | collective-permute-start | bytes 196616 | tf_op jit(solution)/shard_map/ppermute | solution.py:153
  17.3 2.0 %collective-permute-start.4 = (bf16[32,1024]{1,0:T(8,128)(2,1)S(1)}, bf16[32,1024]{1,0:T(8,128)(2,1)S(1)}, u32[]{:S(2)}, u32[]{:S(2)}) collective-permute-start(bf16[32,1024]{1,0:T(8,128)(2,1)S(1)} %add_convert_fusion.refs_0_), channel_id=1, source_target_pairs={{0,8},{4,12},{8,0},{12,4},{1,9},{5,13},{9,1},{13,5},{2,10},{6,14},... | collective-permute-start | bytes 196616 | tf_op jit(solution)/shard_map/ppermute | solution.py:153
  19.3 2.2 %collective-permute-start.3 = (bf16[32,1024]{1,0:T(8,128)(2,1)S(1)}, bf16[32,1024]{1,0:T(8,128)(2,1)S(1)}, u32[]{:S(2)}, u32[]{:S(2)}) collective-permute-start(bf16[32,1024]{1,0:T(8,128)(2,1)S(1)} %add_convert_fusion.refs_0_), channel_id=1, source_target_pairs={{0,12},{4,0},{8,4},{12,8},{1,13},{5,1},{9,5},{13,9},{2,14},{6,2},{... | collective-permute-start | bytes 196616 | tf_op jit(solution)/shard_map/ppermute | solution.py:153
  21.5 0.4 %collective-permute-done.5.refs_1_ = bf16[32,1024]{1,0:T(8,128)(2,1)S(1)} collective-permute-done((bf16[32,1024]{1,0:T(8,128)(2,1)S(1)}, bf16[32,1024]{1,0:T(8,128)(2,1)S(1)}, u32[]{:S(2)}, u32[]{:S(2)}) %collective-permute-start.5) | collective-permute-done | bytes 65568 | tf_op jit(solution)/shard_map/ppermute | solution.py:153
  21.9 0.4 %score.3.refs_2_ = f32[32,256]{1,0:T(8,128)S(1)} custom-call(bf16[32,1024]{1,0:T(8,128)(2,1)S(1)} %add_convert_fusion.refs_0_, bf16[32,1024]{1,0:T(8,128)(2,1)S(1)} %collective-permute-done.5.refs_1_, bf16[1,256,4096]{2,1,0:T(8,128)(2,1)S(1)} %copy-done), custom_call_target="tpu_custom_call" | custom-call | flops 33554432 | bytes 1048576 | tf_op jit(solution)/shard_map/score/pallas_call | solution.py:138
  22.3 0.4 %collective-permute-done.4.refs_0_ = bf16[32,1024]{1,0:T(8,128)(2,1)S(1)} collective-permute-done((bf16[32,1024]{1,0:T(8,128)(2,1)S(1)}, bf16[32,1024]{1,0:T(8,128)(2,1)S(1)}, u32[]{:S(2)}, u32[]{:S(2)}) %collective-permute-start.4) | collective-permute-done | bytes 65568 | tf_op jit(solution)/shard_map/ppermute | solution.py:153
  22.8 0.2 score.4.refs_2_
  23.0 0.6 %collective-permute-done.3.refs_0_ = bf16[32,1024]{1,0:T(8,128)(2,1)S(1)} collective-permute-done((bf16[32,1024]{1,0:T(8,128)(2,1)S(1)}, bf16[32,1024]{1,0:T(8,128)(2,1)S(1)}, u32[]{:S(2)}, u32[]{:S(2)}) %collective-permute-start.3) | collective-permute-done | bytes 65568 | tf_op jit(solution)/shard_map/ppermute | solution.py:153
  23.6 0.3 score.5
  23.9 0.1 collective-permute-start.6
  23.9 1.6 %collective-permute-start.7 = (f32[8,256]{1,0:T(8,128)S(1)}, f32[8,256]{1,0:T(8,128)S(1)}, u32[]{:S(2)}, u32[]{:S(2)}) collective-permute-start(f32[8,256]{1,0:T(8,128)S(1)} %get-tuple-element.17), channel_id=1, source_target_pairs={{0,1},{1,0},{2,3},{3,2},{4,5},{5,4},{6,7},{7,6},{8,9},{9,8},{10,11... | collective-permute-start | bytes 24584 | tf_op jit(solution)/shard_map/ppermute | solution.py:153
  25.5 0.3 %collective-permute-start.8 = (f32[8,256]{1,0:T(8,128)S(1)}, f32[8,256]{1,0:T(8,128)S(1)}, u32[]{:S(2)}, u32[]{:S(2)}) collective-permute-start(f32[8,256]{1,0:T(8,128)S(1)} %get-tuple-element.18), channel_id=1, source_target_pairs={{0,2},{1,3},{2,0},{3,1},{4,6},{5,7},{6,4},{7,5},{8,10},{9,11},{10,... | collective-permute-start | bytes 24584 | tf_op jit(solution)/shard_map/ppermute | solution.py:153
  25.8 1.3 %collective-permute-done.6 = f32[8,256]{1,0:T(8,128)S(1)} collective-permute-done((f32[8,256]{1,0:T(8,128)S(1)}, f32[8,256]{1,0:T(8,128)S(1)}, u32[]{:S(2)}, u32[]{:S(2)}) %collective-permute-start.6) | collective-permute-done | bytes 8224 | tf_op jit(solution)/shard_map/ppermute | solution.py:153
  27.0 0.6 %collective-permute-done.7 = f32[8,256]{1,0:T(8,128)S(1)} collective-permute-done((f32[8,256]{1,0:T(8,128)S(1)}, f32[8,256]{1,0:T(8,128)S(1)}, u32[]{:S(2)}, u32[]{:S(2)}) %collective-permute-start.7) | collective-permute-done | bytes 8224 | tf_op jit(solution)/shard_map/ppermute | solution.py:153
  27.7 0.0 collective-permute-done.8
  27.7 0.6 %add_add_fusion = f32[8,256]{1,0:T(8,128)} fusion(f32[8,256]{1,0:T(8,128)S(1)} %collective-permute-done.8, f32[8,256]{1,0:T(8,128)S(1)} %collective-permute-done.7, f32[8,256]{1,0:T(8,128)S(1)} %get-tuple-element.15, f32[8,256]{1,0:T(8,128)S(1)} %collective-permute-done.6), kind=kLoop, calls=%fused_computation.1 | loop fusion | flops 6144 | bytes 40960 | tf_op jit(solution)/shard_map/add | solution.py:173
  (5 shorter events, 0.0 us)
Async XLA Ops:
  0.0 21.9 %copy-start = (bf16[1,256,4096]{2,1,0:T(8,128)(2,1)S(1)}, bf16[1,256,4096]{2,1,0:T(8,128)(2,1)}, u32[]{:S(2)}) copy-start(bf16[1,256,4096]{2,1,0:T(8,128)(2,1)} %refs_1_.3) | copy-start | bytes 6291460
  0.0 23.6 %copy-start.1 = (f32[1,256]{1,0:T(1,128)S(1)}, f32[1,256]{1,0:T(1,128)}, u32[]{:S(2)}) copy-start(f32[1,256]{1,0:T(1,128)} %refs_3_.1) | copy-start | bytes 3076
  5.3 9.7 %collective-permute-start = (bf16[32,1024]{1,0:T(8,128)(2,1)S(1)}, bf16[32,1024]{1,0:T(8,128)(2,1)S(1)}, u32[]{:S(2)}, u32[]{:S(2)}) collective-permute-start(bf16[32,1024]{1,0:T(8,128)(2,1)S(1)} %get-tuple-element.12), channel_id=1, source_target_pairs={{0,4},{4,12},{8,0},{12,8},{1,5},{5,13},{9,1},{13,9},{2,6},{6,14},{... | collective-permute-start | bytes 196616 | tf_op jit(solution)/shard_map/ppermute | solution.py:153
  8.4 7.0 %collective-permute-start.1 = (bf16[32,1024]{1,0:T(8,128)(2,1)S(1)}, bf16[32,1024]{1,0:T(8,128)(2,1)S(1)}, u32[]{:S(2)}, u32[]{:S(2)}) collective-permute-start(bf16[32,1024]{1,0:T(8,128)(2,1)S(1)} %get-tuple-element.13), channel_id=1, source_target_pairs={{0,12},{4,8},{8,4},{12,0},{1,13},{5,9},{9,5},{13,1},{2,14},{6,10},... | collective-permute-start | bytes 196616 | tf_op jit(solution)/shard_map/ppermute | solution.py:153
  10.9 4.7 %collective-permute-start.2 = (bf16[32,1024]{1,0:T(8,128)(2,1)S(1)}, bf16[32,1024]{1,0:T(8,128)(2,1)S(1)}, u32[]{:S(2)}, u32[]{:S(2)}) collective-permute-start(bf16[32,1024]{1,0:T(8,128)(2,1)S(1)} %get-tuple-element.14), channel_id=1, source_target_pairs={{0,8},{4,0},{8,12},{12,4},{1,9},{5,1},{9,13},{13,5},{2,10},{6,2},{... | collective-permute-start | bytes 196616 | tf_op jit(solution)/shard_map/ppermute | solution.py:153
  15.6 6.3 %collective-permute-start.5 = (bf16[32,1024]{1,0:T(8,128)(2,1)S(1)}, bf16[32,1024]{1,0:T(8,128)(2,1)S(1)}, u32[]{:S(2)}, u32[]{:S(2)}) collective-permute-start(bf16[32,1024]{1,0:T(8,128)(2,1)S(1)} %add_convert_fusion.refs_0_), channel_id=1, source_target_pairs={{0,4},{4,8},{8,12},{12,0},{1,5},{5,9},{9,13},{13,1},{2,6},{6,10},{... | collective-permute-start | bytes 196616 | tf_op jit(solution)/shard_map/ppermute | solution.py:153
  17.3 5.5 %collective-permute-start.4 = (bf16[32,1024]{1,0:T(8,128)(2,1)S(1)}, bf16[32,1024]{1,0:T(8,128)(2,1)S(1)}, u32[]{:S(2)}, u32[]{:S(2)}) collective-permute-start(bf16[32,1024]{1,0:T(8,128)(2,1)S(1)} %add_convert_fusion.refs_0_), channel_id=1, source_target_pairs={{0,8},{4,12},{8,0},{12,4},{1,9},{5,13},{9,1},{13,5},{2,10},{6,14},... | collective-permute-start | bytes 196616 | tf_op jit(solution)/shard_map/ppermute | solution.py:153
  19.3 4.3 %collective-permute-start.3 = (bf16[32,1024]{1,0:T(8,128)(2,1)S(1)}, bf16[32,1024]{1,0:T(8,128)(2,1)S(1)}, u32[]{:S(2)}, u32[]{:S(2)}) collective-permute-start(bf16[32,1024]{1,0:T(8,128)(2,1)S(1)} %add_convert_fusion.refs_0_), channel_id=1, source_target_pairs={{0,12},{4,0},{8,4},{12,8},{1,13},{5,1},{9,5},{13,9},{2,14},{6,2},{... | collective-permute-start | bytes 196616 | tf_op jit(solution)/shard_map/ppermute | solution.py:153
  23.9 3.2 %collective-permute-start.6 = (f32[8,256]{1,0:T(8,128)S(1)}, f32[8,256]{1,0:T(8,128)S(1)}, u32[]{:S(2)}, u32[]{:S(2)}) collective-permute-start(f32[8,256]{1,0:T(8,128)S(1)} %get-tuple-element.16), channel_id=1, source_target_pairs={{0,3},{1,2},{2,1},{3,0},{4,7},{5,6},{6,5},{7,4},{8,11},{9,10},{10,... | collective-permute-start | bytes 24584 | tf_op jit(solution)/shard_map/ppermute | solution.py:153
  23.9 3.7 %collective-permute-start.7 = (f32[8,256]{1,0:T(8,128)S(1)}, f32[8,256]{1,0:T(8,128)S(1)}, u32[]{:S(2)}, u32[]{:S(2)}) collective-permute-start(f32[8,256]{1,0:T(8,128)S(1)} %get-tuple-element.17), channel_id=1, source_target_pairs={{0,1},{1,0},{2,3},{3,2},{4,5},{5,4},{6,7},{7,6},{8,9},{9,8},{10,11... | collective-permute-start | bytes 24584 | tf_op jit(solution)/shard_map/ppermute | solution.py:153
  25.5 2.2 %collective-permute-start.8 = (f32[8,256]{1,0:T(8,128)S(1)}, f32[8,256]{1,0:T(8,128)S(1)}, u32[]{:S(2)}, u32[]{:S(2)}) collective-permute-start(f32[8,256]{1,0:T(8,128)S(1)} %get-tuple-element.18), channel_id=1, source_target_pairs={{0,2},{1,3},{2,0},{3,1},{4,6},{5,7},{6,4},{7,5},{8,10},{9,11},{10,... | collective-permute-start | bytes 24584 | tf_op jit(solution)/shard_map/ppermute | solution.py:153

commit v7 on v6

--- a/solution.py
+++ b/solution.py
@@ -158,8 +158,7 @@
     away = project(n, out_tables, jnp.bfloat16, test_feat, kernel_inverse)
     terms = [send(block, "dp", table) for table, block in zip(out_tables, away)]
     (total,) = project(n, [], jnp.float32, test_feat, kernel_inverse)
-    for term in terms:
-        total = total + term
+    total = sum(terms[1:], terms[0].astype(jnp.float32)) + total
     total = total.astype(jnp.bfloat16)
     back_tables = [plain_ring(n, step) for step in range(1, n)]
     blocks = [total] + [send(total, "dp", table) for table in back_tables]

time: 28.4 us -> 28.4 us (level)
  no operation moved by 1% of the time
where the time goes in v7:
time: 28.4 us; the launch traced here: 28.3 us
  starting transfers between devices  14.9 us (52%)
  Pallas kernels  8.79 us (31%)
  waiting for transfers between devices  3.84 us (14%)
  other arithmetic  0.64 us (2%)
    ppermute x9, starting transfers between devices, send(): return lax.ppermute(x, axes, list(enumerate(table)))  14.9 us
    pallas_call x2, Pallas kernels, project(): pl.pallas_call(functools.partial(project_kernel, n, tables, cuts), in_spe...  7.88 us
    ppermute x9, waiting for transfers between devices, send(): return lax.ppermute(x, axes, list(enumerate(table)))  3.84 us
    pallas_call x3, Pallas kernels, score(): pl.pallas_call(functools.partial(score_kernel, tables, parts, axes), in_s...  0.91 us
    add x1, other arithmetic, line_shards(): result = result + send(rows[step], axes, [z ^ step for z in range(parts)])  0.6 us
  transfers between devices with their start and end apart: 9, of which 7 were waited for; matrix products, arithmetic and copies ran while one was open for 0% of the time, Pallas kernels for 11%

profile of v7, /device:TPU:0, one launch (start us, length us, event | category | flops | bytes accessed | tf_op | source)
XLA Modules:
  0.0 28.3 jit_solution(11116626342508987857)
XLA Ops:
  0.0 5.3 %project.2 = (bf16[32,1024]{1,0:T(8,128)(2,1)S(1)}, bf16[32,1024]{1,0:T(8,128)(2,1)S(1)}, bf16[32,1024]{1,0:T(8,128)(2,1)S(1)}) custom-call(bf16[1,32,2048]{2,1,0:T(8,128)(2,1)} %test_ref.3, bf16[1,2048,4096]{2,1,0:T(8,128)(2,1)} %inverse_ref.3), custom_call_target="tpu_custom_call" | custom-call | flops 402653184 | bytes 12582912 | tf_op jit(solution)/shard_map/project/pallas_call | solution.py:91
  5.3 3.1 %collective-permute-start = (bf16[32,1024]{1,0:T(8,128)(2,1)S(1)}, bf16[32,1024]{1,0:T(8,128)(2,1)S(1)}, u32[]{:S(2)}, u32[]{:S(2)}) collective-permute-start(bf16[32,1024]{1,0:T(8,128)(2,1)S(1)} %get-tuple-element.12), channel_id=1, source_target_pairs={{0,4},{4,12},{8,0},{12,8},{1,5},{5,13},{9,1},{13,9},{2,6},{6,14},{... | collective-permute-start | bytes 196616 | tf_op jit(solution)/shard_map/ppermute | solution.py:153
  8.4 2.5 %collective-permute-start.1 = (bf16[32,1024]{1,0:T(8,128)(2,1)S(1)}, bf16[32,1024]{1,0:T(8,128)(2,1)S(1)}, u32[]{:S(2)}, u32[]{:S(2)}) collective-permute-start(bf16[32,1024]{1,0:T(8,128)(2,1)S(1)} %get-tuple-element.13), channel_id=1, source_target_pairs={{0,12},{4,8},{8,4},{12,0},{1,13},{5,9},{9,5},{13,1},{2,14},{6,10},... | collective-permute-start | bytes 196616 | tf_op jit(solution)/shard_map/ppermute | solution.py:153
  10.9 1.6 %collective-permute-start.2 = (bf16[32,1024]{1,0:T(8,128)(2,1)S(1)}, bf16[32,1024]{1,0:T(8,128)(2,1)S(1)}, u32[]{:S(2)}, u32[]{:S(2)}) collective-permute-start(bf16[32,1024]{1,0:T(8,128)(2,1)S(1)} %get-tuple-element.14), channel_id=1, source_target_pairs={{0,8},{4,0},{8,12},{12,4},{1,9},{5,1},{9,13},{13,5},{2,10},{6,2},{... | collective-permute-start | bytes 196616 | tf_op jit(solution)/shard_map/ppermute | solution.py:153
  12.4 2.6 %project.3 = f32[32,1024]{1,0:T(8,128)S(1)} custom-call(bf16[1,32,2048]{2,1,0:T(8,128)(2,1)} %test_ref.3, bf16[1,2048,4096]{2,1,0:T(8,128)(2,1)} %inverse_ref.3), custom_call_target="tpu_custom_call" | custom-call | flops 134217728 | bytes 4194304 | tf_op jit(solution)/shard_map/project/pallas_call | solution.py:91
  15.0 0.0 collective-permute-done
  15.0 0.3 %collective-permute-done.1 = bf16[32,1024]{1,0:T(8,128)(2,1)S(1)} collective-permute-done((bf16[32,1024]{1,0:T(8,128)(2,1)S(1)}, bf16[32,1024]{1,0:T(8,128)(2,1)S(1)}, u32[]{:S(2)}, u32[]{:S(2)}) %collective-permute-start.1) | collective-permute-done | bytes 65568 | tf_op jit(solution)/shard_map/ppermute | solution.py:153
  15.3 0.2 collective-permute-done.2
  15.6 1.7 %collective-permute-start.5 = (bf16[32,1024]{1,0:T(8,128)(2,1)S(1)}, bf16[32,1024]{1,0:T(8,128)(2,1)S(1)}, u32[]{:S(2)}, u32[]{:S(2)}) collective-permute-start(bf16[32,1024]{1,0:T(8,128)(2,1)S(1)} %add_convert_fusion.refs_0_), channel_id=1, source_target_pairs={{0,4},{4,8},{8,12},{12,0},{1,5},{5,9},{9,13},{13,1},{2,6},{6,10},{... | collective-permute-start | bytes 196616 | tf_op jit(solution)/shard_map/ppermute | solution.py:153
  17.3 2.0 %collective-permute-start.4 = (bf16[32,1024]{1,0:T(8,128)(2,1)S(1)}, bf16[32,1024]{1,0:T(8,128)(2,1)S(1)}, u32[]{:S(2)}, u32[]{:S(2)}) collective-permute-start(bf16[32,1024]{1,0:T(8,128)(2,1)S(1)} %add_convert_fusion.refs_0_), channel_id=1, source_target_pairs={{0,8},{4,12},{8,0},{12,4},{1,9},{5,13},{9,1},{13,5},{2,10},{6,14},... | collective-permute-start | bytes 196616 | tf_op jit(solution)/shard_map/ppermute | solution.py:153
  19.3 2.2 %collective-permute-start.3 = (bf16[32,1024]{1,0:T(8,128)(2,1)S(1)}, bf16[32,1024]{1,0:T(8,128)(2,1)S(1)}, u32[]{:S(2)}, u32[]{:S(2)}) collective-permute-start(bf16[32,1024]{1,0:T(8,128)(2,1)S(1)} %add_convert_fusion.refs_0_), channel_id=1, source_target_pairs={{0,12},{4,0},{8,4},{12,8},{1,13},{5,1},{9,5},{13,9},{2,14},{6,2},{... | collective-permute-start | bytes 196616 | tf_op jit(solution)/shard_map/ppermute | solution.py:153
  21.5 0.4 %collective-permute-done.5.refs_1_ = bf16[32,1024]{1,0:T(8,128)(2,1)S(1)} collective-permute-done((bf16[32,1024]{1,0:T(8,128)(2,1)S(1)}, bf16[32,1024]{1,0:T(8,128)(2,1)S(1)}, u32[]{:S(2)}, u32[]{:S(2)}) %collective-permute-start.5) | collective-permute-done | bytes 65568 | tf_op jit(solution)/shard_map/ppermute | solution.py:153
  21.9 0.4 %score.3.refs_2_ = f32[32,256]{1,0:T(8,128)S(1)} custom-call(bf16[32,1024]{1,0:T(8,128)(2,1)S(1)} %add_convert_fusion.refs_0_, bf16[32,1024]{1,0:T(8,128)(2,1)S(1)} %collective-permute-done.5.refs_1_, bf16[1,256,4096]{2,1,0:T(8,128)(2,1)S(1)} %copy-done), custom_call_target="tpu_custom_call" | custom-call | flops 33554432 | bytes 1048576 | tf_op jit(solution)/shard_map/score/pallas_call | solution.py:138
  22.3 0.4 %collective-permute-done.4.refs_0_ = bf16[32,1024]{1,0:T(8,128)(2,1)S(1)} collective-permute-done((bf16[32,1024]{1,0:T(8,128)(2,1)S(1)}, bf16[32,1024]{1,0:T(8,128)(2,1)S(1)}, u32[]{:S(2)}, u32[]{:S(2)}) %collective-permute-start.4) | collective-permute-done | bytes 65568 | tf_op jit(solution)/shard_map/ppermute | solution.py:153
  22.8 0.2 score.4.refs_2_
  23.0 0.6 %collective-permute-done.3.refs_0_ = bf16[32,1024]{1,0:T(8,128)(2,1)S(1)} collective-permute-done((bf16[32,1024]{1,0:T(8,128)(2,1)S(1)}, bf16[32,1024]{1,0:T(8,128)(2,1)S(1)}, u32[]{:S(2)}, u32[]{:S(2)}) %collective-permute-start.3) | collective-permute-done | bytes 65568 | tf_op jit(solution)/shard_map/ppermute | solution.py:153
  23.6 0.3 score.5
  23.9 0.1 collective-permute-start.6
  23.9 1.6 %collective-permute-start.7 = (f32[8,256]{1,0:T(8,128)S(1)}, f32[8,256]{1,0:T(8,128)S(1)}, u32[]{:S(2)}, u32[]{:S(2)}) collective-permute-start(f32[8,256]{1,0:T(8,128)S(1)} %get-tuple-element.17), channel_id=1, source_target_pairs={{0,1},{1,0},{2,3},{3,2},{4,5},{5,4},{6,7},{7,6},{8,9},{9,8},{10,11... | collective-permute-start | bytes 24584 | tf_op jit(solution)/shard_map/ppermute | solution.py:153
  25.5 0.3 %collective-permute-start.8 = (f32[8,256]{1,0:T(8,128)S(1)}, f32[8,256]{1,0:T(8,128)S(1)}, u32[]{:S(2)}, u32[]{:S(2)}) collective-permute-start(f32[8,256]{1,0:T(8,128)S(1)} %get-tuple-element.18), channel_id=1, source_target_pairs={{0,2},{1,3},{2,0},{3,1},{4,6},{5,7},{6,4},{7,5},{8,10},{9,11},{10,... | collective-permute-start | bytes 24584 | tf_op jit(solution)/shard_map/ppermute | solution.py:153
  25.8 1.3 %collective-permute-done.6 = f32[8,256]{1,0:T(8,128)S(1)} collective-permute-done((f32[8,256]{1,0:T(8,128)S(1)}, f32[8,256]{1,0:T(8,128)S(1)}, u32[]{:S(2)}, u32[]{:S(2)}) %collective-permute-start.6) | collective-permute-done | bytes 8224 | tf_op jit(solution)/shard_map/ppermute | solution.py:153
  27.0 0.6 %collective-permute-done.7 = f32[8,256]{1,0:T(8,128)S(1)} collective-permute-done((f32[8,256]{1,0:T(8,128)S(1)}, f32[8,256]{1,0:T(8,128)S(1)}, u32[]{:S(2)}, u32[]{:S(2)}) %collective-permute-start.7) | collective-permute-done | bytes 8224 | tf_op jit(solution)/shard_map/ppermute | solution.py:153
  27.7 0.0 collective-permute-done.8
  27.7 0.6 %add_add_fusion = f32[8,256]{1,0:T(8,128)} fusion(f32[8,256]{1,0:T(8,128)S(1)} %collective-permute-done.8, f32[8,256]{1,0:T(8,128)S(1)} %collective-permute-done.7, f32[8,256]{1,0:T(8,128)S(1)} %get-tuple-element.15, f32[8,256]{1,0:T(8,128)S(1)} %collective-permute-done.6), kind=kLoop, calls=%fused_computation.1 | loop fusion | flops 6144 | bytes 40960 | tf_op jit(solution)/shard_map/add | solution.py:172
  (5 shorter events, 0.0 us)
Async XLA Ops:
  0.0 21.9 %copy-start = (bf16[1,256,4096]{2,1,0:T(8,128)(2,1)S(1)}, bf16[1,256,4096]{2,1,0:T(8,128)(2,1)}, u32[]{:S(2)}) copy-start(bf16[1,256,4096]{2,1,0:T(8,128)(2,1)} %refs_1_.3) | copy-start | bytes 6291460
  0.0 23.6 %copy-start.1 = (f32[1,256]{1,0:T(1,128)S(1)}, f32[1,256]{1,0:T(1,128)}, u32[]{:S(2)}) copy-start(f32[1,256]{1,0:T(1,128)} %refs_3_.1) | copy-start | bytes 3076
  5.3 9.7 %collective-permute-start = (bf16[32,1024]{1,0:T(8,128)(2,1)S(1)}, bf16[32,1024]{1,0:T(8,128)(2,1)S(1)}, u32[]{:S(2)}, u32[]{:S(2)}) collective-permute-start(bf16[32,1024]{1,0:T(8,128)(2,1)S(1)} %get-tuple-element.12), channel_id=1, source_target_pairs={{0,4},{4,12},{8,0},{12,8},{1,5},{5,13},{9,1},{13,9},{2,6},{6,14},{... | collective-permute-start | bytes 196616 | tf_op jit(solution)/shard_map/ppermute | solution.py:153
  8.4 7.0 %collective-permute-start.1 = (bf16[32,1024]{1,0:T(8,128)(2,1)S(1)}, bf16[32,1024]{1,0:T(8,128)(2,1)S(1)}, u32[]{:S(2)}, u32[]{:S(2)}) collective-permute-start(bf16[32,1024]{1,0:T(8,128)(2,1)S(1)} %get-tuple-element.13), channel_id=1, source_target_pairs={{0,12},{4,8},{8,4},{12,0},{1,13},{5,9},{9,5},{13,1},{2,14},{6,10},... | collective-permute-start | bytes 196616 | tf_op jit(solution)/shard_map/ppermute | solution.py:153
  10.9 4.7 %collective-permute-start.2 = (bf16[32,1024]{1,0:T(8,128)(2,1)S(1)}, bf16[32,1024]{1,0:T(8,128)(2,1)S(1)}, u32[]{:S(2)}, u32[]{:S(2)}) collective-permute-start(bf16[32,1024]{1,0:T(8,128)(2,1)S(1)} %get-tuple-element.14), channel_id=1, source_target_pairs={{0,8},{4,0},{8,12},{12,4},{1,9},{5,1},{9,13},{13,5},{2,10},{6,2},{... | collective-permute-start | bytes 196616 | tf_op jit(solution)/shard_map/ppermute | solution.py:153
  15.6 6.3 %collective-permute-start.5 = (bf16[32,1024]{1,0:T(8,128)(2,1)S(1)}, bf16[32,1024]{1,0:T(8,128)(2,1)S(1)}, u32[]{:S(2)}, u32[]{:S(2)}) collective-permute-start(bf16[32,1024]{1,0:T(8,128)(2,1)S(1)} %add_convert_fusion.refs_0_), channel_id=1, source_target_pairs={{0,4},{4,8},{8,12},{12,0},{1,5},{5,9},{9,13},{13,1},{2,6},{6,10},{... | collective-permute-start | bytes 196616 | tf_op jit(solution)/shard_map/ppermute | solution.py:153
  17.3 5.5 %collective-permute-start.4 = (bf16[32,1024]{1,0:T(8,128)(2,1)S(1)}, bf16[32,1024]{1,0:T(8,128)(2,1)S(1)}, u32[]{:S(2)}, u32[]{:S(2)}) collective-permute-start(bf16[32,1024]{1,0:T(8,128)(2,1)S(1)} %add_convert_fusion.refs_0_), channel_id=1, source_target_pairs={{0,8},{4,12},{8,0},{12,4},{1,9},{5,13},{9,1},{13,5},{2,10},{6,14},... | collective-permute-start | bytes 196616 | tf_op jit(solution)/shard_map/ppermute | solution.py:153
  19.3 4.3 %collective-permute-start.3 = (bf16[32,1024]{1,0:T(8,128)(2,1)S(1)}, bf16[32,1024]{1,0:T(8,128)(2,1)S(1)}, u32[]{:S(2)}, u32[]{:S(2)}) collective-permute-start(bf16[32,1024]{1,0:T(8,128)(2,1)S(1)} %add_convert_fusion.refs_0_), channel_id=1, source_target_pairs={{0,12},{4,0},{8,4},{12,8},{1,13},{5,1},{9,5},{13,9},{2,14},{6,2},{... | collective-permute-start | bytes 196616 | tf_op jit(solution)/shard_map/ppermute | solution.py:153
  23.9 3.2 %collective-permute-start.6 = (f32[8,256]{1,0:T(8,128)S(1)}, f32[8,256]{1,0:T(8,128)S(1)}, u32[]{:S(2)}, u32[]{:S(2)}) collective-permute-start(f32[8,256]{1,0:T(8,128)S(1)} %get-tuple-element.16), channel_id=1, source_target_pairs={{0,3},{1,2},{2,1},{3,0},{4,7},{5,6},{6,5},{7,4},{8,11},{9,10},{10,... | collective-permute-start | bytes 24584 | tf_op jit(solution)/shard_map/ppermute | solution.py:153
  23.9 3.7 %collective-permute-start.7 = (f32[8,256]{1,0:T(8,128)S(1)}, f32[8,256]{1,0:T(8,128)S(1)}, u32[]{:S(2)}, u32[]{:S(2)}) collective-permute-start(f32[8,256]{1,0:T(8,128)S(1)} %get-tuple-element.17), channel_id=1, source_target_pairs={{0,1},{1,0},{2,3},{3,2},{4,5},{5,4},{6,7},{7,6},{8,9},{9,8},{10,11... | collective-permute-start | bytes 24584 | tf_op jit(solution)/shard_map/ppermute | solution.py:153
  25.5 2.2 %collective-permute-start.8 = (f32[8,256]{1,0:T(8,128)S(1)}, f32[8,256]{1,0:T(8,128)S(1)}, u32[]{:S(2)}, u32[]{:S(2)}) collective-permute-start(f32[8,256]{1,0:T(8,128)S(1)} %get-tuple-element.18), channel_id=1, source_target_pairs={{0,2},{1,3},{2,0},{3,1},{4,6},{5,7},{6,4},{7,5},{8,10},{9,11},{10,... | collective-permute-start | bytes 24584 | tf_op jit(solution)/shard_map/ppermute | solution.py:153

commit v8 on v6

--- a/solution.py
+++ b/solution.py
@@ -164,8 +164,8 @@
     back_tables = [plain_ring(n, step) for step in range(1, n)]
     blocks = [total] + [send(total, "dp", table) for table in back_tables]
     owners = [plain_ring(n, 0)] + [sources(table) for table in back_tables]
-    (raw,) = score(owners[:2], 0, axes, blocks[:2], train_feat)
-    for i in range(2, n - 1):
+    (raw,) = score(owners[:1], 0, axes, blocks[:1], train_feat)
+    for i in range(1, n - 1):
         (raw,) = score(owners[i : i + 1], 0, axes, blocks[i : i + 1], train_feat, raw)
     rows = score(owners[n - 1 :], parts, axes, blocks[n - 1 :], train_feat, raw, residual_weight)
     result = rows[0]

time: 28.4 us -> 28.4 us (level)
    pallas_call x3 -> x4, Pallas kernels: 0.91 us -> 0.97 us  [score(): pl.pallas_call(functools.partial(score_kernel, tables, parts, axes), in_s...]
  transfers between devices with their start and end apart: 9 -> 9, of which waited for: 7 -> 7; matrix products, arithmetic and copies ran while one was open for 0% -> 0% of each run, Pallas kernels for 11% -> 12%
where the time goes in v8:
time: 28.4 us; the launch traced here: 28.3 us
  starting transfers between devices  14.9 us (52%)
  Pallas kernels  8.85 us (31%)
  waiting for transfers between devices  3.79 us (13%)
  other arithmetic  0.64 us (2%)
    ppermute x9, starting transfers between devices, send(): return lax.ppermute(x, axes, list(enumerate(table)))  14.9 us
    pallas_call x2, Pallas kernels, project(): pl.pallas_call(functools.partial(project_kernel, n, tables, cuts), in_spe...  7.88 us
    ppermute x9, waiting for transfers between devices, send(): return lax.ppermute(x, axes, list(enumerate(table)))  3.79 us
    pallas_call x4, Pallas kernels, score(): pl.pallas_call(functools.partial(score_kernel, tables, parts, axes), in_s...  0.97 us
    add x1, other arithmetic, line_shards(): result = result + send(rows[step], axes, [z ^ step for z in range(parts)])  0.6 us
  transfers between devices with their start and end apart: 9, of which 7 were waited for; matrix products, arithmetic and copies ran while one was open for 0% of the time, Pallas kernels for 12%

profile of v8, /device:TPU:0, one launch (start us, length us, event | category | flops | bytes accessed | tf_op | source)
XLA Modules:
  0.0 28.3 jit_solution(57152371782387639)
XLA Ops:
  0.0 5.3 %project.3 = (bf16[32,1024]{1,0:T(8,128)(2,1)S(1)}, bf16[32,1024]{1,0:T(8,128)(2,1)S(1)}, bf16[32,1024]{1,0:T(8,128)(2,1)S(1)}) custom-call(bf16[1,32,2048]{2,1,0:T(8,128)(2,1)} %test_ref.3, bf16[1,2048,4096]{2,1,0:T(8,128)(2,1)} %inverse_ref.3), custom_call_target="tpu_custom_call" | custom-call | flops 402653184 | bytes 12582912 | tf_op jit(solution)/shard_map/project/pallas_call | solution.py:91
  5.3 3.1 %collective-permute-start = (bf16[32,1024]{1,0:T(8,128)(2,1)S(1)}, bf16[32,1024]{1,0:T(8,128)(2,1)S(1)}, u32[]{:S(2)}, u32[]{:S(2)}) collective-permute-start(bf16[32,1024]{1,0:T(8,128)(2,1)S(1)} %get-tuple-element.12), channel_id=1, source_target_pairs={{0,4},{4,12},{8,0},{12,8},{1,5},{5,13},{9,1},{13,9},{2,6},{6,14},{... | collective-permute-start | bytes 196616 | tf_op jit(solution)/shard_map/ppermute | solution.py:153
  8.4 2.5 %collective-permute-start.1 = (bf16[32,1024]{1,0:T(8,128)(2,1)S(1)}, bf16[32,1024]{1,0:T(8,128)(2,1)S(1)}, u32[]{:S(2)}, u32[]{:S(2)}) collective-permute-start(bf16[32,1024]{1,0:T(8,128)(2,1)S(1)} %get-tuple-element.13), channel_id=1, source_target_pairs={{0,12},{4,8},{8,4},{12,0},{1,13},{5,9},{9,5},{13,1},{2,14},{6,10},... | collective-permute-start | bytes 196616 | tf_op jit(solution)/shard_map/ppermute | solution.py:153
  10.9 1.6 %collective-permute-start.2 = (bf16[32,1024]{1,0:T(8,128)(2,1)S(1)}, bf16[32,1024]{1,0:T(8,128)(2,1)S(1)}, u32[]{:S(2)}, u32[]{:S(2)}) collective-permute-start(bf16[32,1024]{1,0:T(8,128)(2,1)S(1)} %get-tuple-element.14), channel_id=1, source_target_pairs={{0,8},{4,0},{8,12},{12,4},{1,9},{5,1},{9,13},{13,5},{2,10},{6,2},{... | collective-permute-start | bytes 196616 | tf_op jit(solution)/shard_map/ppermute | solution.py:153
  12.4 2.6 %project.2 = f32[32,1024]{1,0:T(8,128)S(1)} custom-call(bf16[1,32,2048]{2,1,0:T(8,128)(2,1)} %test_ref.3, bf16[1,2048,4096]{2,1,0:T(8,128)(2,1)} %inverse_ref.3), custom_call_target="tpu_custom_call" | custom-call | flops 134217728 | bytes 4194304 | tf_op jit(solution)/shard_map/project/pallas_call | solution.py:91
  15.0 0.3 %collective-permute-done.1 = bf16[32,1024]{1,0:T(8,128)(2,1)S(1)} collective-permute-done((bf16[32,1024]{1,0:T(8,128)(2,1)S(1)}, bf16[32,1024]{1,0:T(8,128)(2,1)S(1)}, u32[]{:S(2)}, u32[]{:S(2)}) %collective-permute-start.1) | collective-permute-done | bytes 65568 | tf_op jit(solution)/shard_map/ppermute | solution.py:153
  15.3 0.2 collective-permute-done.2
  15.6 1.7 %collective-permute-start.5 = (bf16[32,1024]{1,0:T(8,128)(2,1)S(1)}, bf16[32,1024]{1,0:T(8,128)(2,1)S(1)}, u32[]{:S(2)}, u32[]{:S(2)}) collective-permute-start(bf16[32,1024]{1,0:T(8,128)(2,1)S(1)} %add_convert_fusion.refs_0_), channel_id=1, source_target_pairs={{0,4},{4,8},{8,12},{12,0},{1,5},{5,9},{9,13},{13,1},{2,6},{6,10},{... | collective-permute-start | bytes 196616 | tf_op jit(solution)/shard_map/ppermute | solution.py:153
  17.3 2.0 %collective-permute-start.4 = (bf16[32,1024]{1,0:T(8,128)(2,1)S(1)}, bf16[32,1024]{1,0:T(8,128)(2,1)S(1)}, u32[]{:S(2)}, u32[]{:S(2)}) collective-permute-start(bf16[32,1024]{1,0:T(8,128)(2,1)S(1)} %add_convert_fusion.refs_0_), channel_id=1, source_target_pairs={{0,8},{4,12},{8,0},{12,4},{1,9},{5,13},{9,1},{13,5},{2,10},{6,14},... | collective-permute-start | bytes 196616 | tf_op jit(solution)/shard_map/ppermute | solution.py:153
  19.3 2.2 %collective-permute-start.3 = (bf16[32,1024]{1,0:T(8,128)(2,1)S(1)}, bf16[32,1024]{1,0:T(8,128)(2,1)S(1)}, u32[]{:S(2)}, u32[]{:S(2)}) collective-permute-start(bf16[32,1024]{1,0:T(8,128)(2,1)S(1)} %add_convert_fusion.refs_0_), channel_id=1, source_target_pairs={{0,12},{4,0},{8,4},{12,8},{1,13},{5,1},{9,5},{13,9},{2,14},{6,2},{... | collective-permute-start | bytes 196616 | tf_op jit(solution)/shard_map/ppermute | solution.py:153
  21.5 0.2 score.4.refs_2_
  21.7 0.2 collective-permute-done.5.refs_0_
  21.9 0.2 score.5.refs_2_
  22.2 0.6 %collective-permute-done.4.refs_0_ = bf16[32,1024]{1,0:T(8,128)(2,1)S(1)} collective-permute-done((bf16[32,1024]{1,0:T(8,128)(2,1)S(1)}, bf16[32,1024]{1,0:T(8,128)(2,1)S(1)}, u32[]{:S(2)}, u32[]{:S(2)}) %collective-permute-start.4) | collective-permute-done | bytes 65568 | tf_op jit(solution)/shard_map/ppermute | solution.py:153
  22.8 0.2 score.6.refs_2_
  23.0 0.6 %collective-permute-done.3.refs_0_ = bf16[32,1024]{1,0:T(8,128)(2,1)S(1)} collective-permute-done((bf16[32,1024]{1,0:T(8,128)(2,1)S(1)}, bf16[32,1024]{1,0:T(8,128)(2,1)S(1)}, u32[]{:S(2)}, u32[]{:S(2)}) %collective-permute-start.3) | collective-permute-done | bytes 65568 | tf_op jit(solution)/shard_map/ppermute | solution.py:153
  23.6 0.3 score.7
  23.9 0.1 collective-permute-start.6
  23.9 1.6 %collective-permute-start.7 = (f32[8,256]{1,0:T(8,128)S(1)}, f32[8,256]{1,0:T(8,128)S(1)}, u32[]{:S(2)}, u32[]{:S(2)}) collective-permute-start(f32[8,256]{1,0:T(8,128)S(1)} %get-tuple-element.17), channel_id=1, source_target_pairs={{0,1},{1,0},{2,3},{3,2},{4,5},{5,4},{6,7},{7,6},{8,9},{9,8},{10,11... | collective-permute-start | bytes 24584 | tf_op jit(solution)/shard_map/ppermute | solution.py:153
  25.5 0.3 %collective-permute-start.8 = (f32[8,256]{1,0:T(8,128)S(1)}, f32[8,256]{1,0:T(8,128)S(1)}, u32[]{:S(2)}, u32[]{:S(2)}) collective-permute-start(f32[8,256]{1,0:T(8,128)S(1)} %get-tuple-element.18), channel_id=1, source_target_pairs={{0,2},{1,3},{2,0},{3,1},{4,6},{5,7},{6,4},{7,5},{8,10},{9,11},{10,... | collective-permute-start | bytes 24584 | tf_op jit(solution)/shard_map/ppermute | solution.py:153
  25.8 1.3 %collective-permute-done.6 = f32[8,256]{1,0:T(8,128)S(1)} collective-permute-done((f32[8,256]{1,0:T(8,128)S(1)}, f32[8,256]{1,0:T(8,128)S(1)}, u32[]{:S(2)}, u32[]{:S(2)}) %collective-permute-start.6) | collective-permute-done | bytes 8224 | tf_op jit(solution)/shard_map/ppermute | solution.py:153
  27.0 0.6 %collective-permute-done.7 = f32[8,256]{1,0:T(8,128)S(1)} collective-permute-done((f32[8,256]{1,0:T(8,128)S(1)}, f32[8,256]{1,0:T(8,128)S(1)}, u32[]{:S(2)}, u32[]{:S(2)}) %collective-permute-start.7) | collective-permute-done | bytes 8224 | tf_op jit(solution)/shard_map/ppermute | solution.py:153
  27.7 0.0 collective-permute-done.8
  27.7 0.6 %add_add_fusion = f32[8,256]{1,0:T(8,128)} fusion(f32[8,256]{1,0:T(8,128)S(1)} %collective-permute-done.8, f32[8,256]{1,0:T(8,128)S(1)} %collective-permute-done.7, f32[8,256]{1,0:T(8,128)S(1)} %get-tuple-element.15, f32[8,256]{1,0:T(8,128)S(1)} %collective-permute-done.6), kind=kLoop, calls=%fused_computation.1 | loop fusion | flops 6144 | bytes 40960 | tf_op jit(solution)/shard_map/add | solution.py:173
  (6 shorter events, 0.0 us)
Async XLA Ops:
  0.0 21.5 %copy-start = (bf16[1,256,4096]{2,1,0:T(8,128)(2,1)S(1)}, bf16[1,256,4096]{2,1,0:T(8,128)(2,1)}, u32[]{:S(2)}) copy-start(bf16[1,256,4096]{2,1,0:T(8,128)(2,1)} %refs_1_.7) | copy-start | bytes 6291460
  0.0 23.6 %copy-start.1 = (f32[1,256]{1,0:T(1,128)S(1)}, f32[1,256]{1,0:T(1,128)}, u32[]{:S(2)}) copy-start(f32[1,256]{1,0:T(1,128)} %refs_3_.1) | copy-start | bytes 3076
  5.3 9.7 %collective-permute-start = (bf16[32,1024]{1,0:T(8,128)(2,1)S(1)}, bf16[32,1024]{1,0:T(8,128)(2,1)S(1)}, u32[]{:S(2)}, u32[]{:S(2)}) collective-permute-start(bf16[32,1024]{1,0:T(8,128)(2,1)S(1)} %get-tuple-element.12), channel_id=1, source_target_pairs={{0,4},{4,12},{8,0},{12,8},{1,5},{5,13},{9,1},{13,9},{2,6},{6,14},{... | collective-permute-start | bytes 196616 | tf_op jit(solution)/shard_map/ppermute | solution.py:153
  8.4 7.0 %collective-permute-start.1 = (bf16[32,1024]{1,0:T(8,128)(2,1)S(1)}, bf16[32,1024]{1,0:T(8,128)(2,1)S(1)}, u32[]{:S(2)}, u32[]{:S(2)}) collective-permute-start(bf16[32,1024]{1,0:T(8,128)(2,1)S(1)} %get-tuple-element.13), channel_id=1, source_target_pairs={{0,12},{4,8},{8,4},{12,0},{1,13},{5,9},{9,5},{13,1},{2,14},{6,10},... | collective-permute-start | bytes 196616 | tf_op jit(solution)/shard_map/ppermute | solution.py:153
  10.9 4.7 %collective-permute-start.2 = (bf16[32,1024]{1,0:T(8,128)(2,1)S(1)}, bf16[32,1024]{1,0:T(8,128)(2,1)S(1)}, u32[]{:S(2)}, u32[]{:S(2)}) collective-permute-start(bf16[32,1024]{1,0:T(8,128)(2,1)S(1)} %get-tuple-element.14), channel_id=1, source_target_pairs={{0,8},{4,0},{8,12},{12,4},{1,9},{5,1},{9,13},{13,5},{2,10},{6,2},{... | collective-permute-start | bytes 196616 | tf_op jit(solution)/shard_map/ppermute | solution.py:153
  15.6 6.3 %collective-permute-start.5 = (bf16[32,1024]{1,0:T(8,128)(2,1)S(1)}, bf16[32,1024]{1,0:T(8,128)(2,1)S(1)}, u32[]{:S(2)}, u32[]{:S(2)}) collective-permute-start(bf16[32,1024]{1,0:T(8,128)(2,1)S(1)} %add_convert_fusion.refs_0_), channel_id=1, source_target_pairs={{0,4},{4,8},{8,12},{12,0},{1,5},{5,9},{9,13},{13,1},{2,6},{6,10},{... | collective-permute-start | bytes 196616 | tf_op jit(solution)/shard_map/ppermute | solution.py:153
  17.3 5.5 %collective-permute-start.4 = (bf16[32,1024]{1,0:T(8,128)(2,1)S(1)}, bf16[32,1024]{1,0:T(8,128)(2,1)S(1)}, u32[]{:S(2)}, u32[]{:S(2)}) collective-permute-start(bf16[32,1024]{1,0:T(8,128)(2,1)S(1)} %add_convert_fusion.refs_0_), channel_id=1, source_target_pairs={{0,8},{4,12},{8,0},{12,4},{1,9},{5,13},{9,1},{13,5},{2,10},{6,14},... | collective-permute-start | bytes 196616 | tf_op jit(solution)/shard_map/ppermute | solution.py:153
  19.3 4.3 %collective-permute-start.3 = (bf16[32,1024]{1,0:T(8,128)(2,1)S(1)}, bf16[32,1024]{1,0:T(8,128)(2,1)S(1)}, u32[]{:S(2)}, u32[]{:S(2)}) collective-permute-start(bf16[32,1024]{1,0:T(8,128)(2,1)S(1)} %add_convert_fusion.refs_0_), channel_id=1, source_target_pairs={{0,12},{4,0},{8,4},{12,8},{1,13},{5,1},{9,5},{13,9},{2,14},{6,2},{... | collective-permute-start | bytes 196616 | tf_op jit(solution)/shard_map/ppermute | solution.py:153
  23.9 3.2 %collective-permute-start.6 = (f32[8,256]{1,0:T(8,128)S(1)}, f32[8,256]{1,0:T(8,128)S(1)}, u32[]{:S(2)}, u32[]{:S(2)}) collective-permute-start(f32[8,256]{1,0:T(8,128)S(1)} %get-tuple-element.16), channel_id=1, source_target_pairs={{0,3},{1,2},{2,1},{3,0},{4,7},{5,6},{6,5},{7,4},{8,11},{9,10},{10,... | collective-permute-start | bytes 24584 | tf_op jit(solution)/shard_map/ppermute | solution.py:153
  23.9 3.7 %collective-permute-start.7 = (f32[8,256]{1,0:T(8,128)S(1)}, f32[8,256]{1,0:T(8,128)S(1)}, u32[]{:S(2)}, u32[]{:S(2)}) collective-permute-start(f32[8,256]{1,0:T(8,128)S(1)} %get-tuple-element.17), channel_id=1, source_target_pairs={{0,1},{1,0},{2,3},{3,2},{4,5},{5,4},{6,7},{7,6},{8,9},{9,8},{10,11... | collective-permute-start | bytes 24584 | tf_op jit(solution)/shard_map/ppermute | solution.py:153
  25.5 2.2 %collective-permute-start.8 = (f32[8,256]{1,0:T(8,128)S(1)}, f32[8,256]{1,0:T(8,128)S(1)}, u32[]{:S(2)}, u32[]{:S(2)}) collective-permute-start(f32[8,256]{1,0:T(8,128)S(1)} %get-tuple-element.18), channel_id=1, source_target_pairs={{0,2},{1,3},{2,0},{3,1},{4,6},{5,7},{6,4},{7,5},{8,10},{9,11},{10,... | collective-permute-start | bytes 24584 | tf_op jit(solution)/shard_map/ppermute | solution.py:153
